TPU v7x, 32 devices: a whole 2x2x4 slice. The times are simulated.
32 devices in a mesh: groups: 2 (over x), surf: 16 (over z, y, core).
Axes of the slice: x: 2, y: 2, z: 4, core: 2. Of those that a mesh axis runs over, the one named last changes fastest.
Arguments:
- sensitivity: bfloat16 [96, 131072], P(None, ('groups', 'surf')), parts along dimension 1, may hold values from -6 to 6
- owner: int32 [131072], P(('groups', 'surf')), parts along dimension 0, may hold values from 0 to 65535, as said below
- patch_count: int32 [32], P(('groups', 'surf')), parts along dimension 0, may hold values from 16 to 32, as said below
- neighbours: int32 [1024, 9], P(('groups', 'surf')), parts along dimension 0, may hold values from 0 to 511, as said below
- coupling: float32 [1024, 9], P(('groups', 'surf')), parts along dimension 0, may hold values from 0.25 to 2
Outputs:
- surface_grad: float32 [96, 131072], P(None, ('groups', 'surf')), parts along dimension 1
- smoothed: float32 [96, 131072], P(None, ('groups', 'surf')), parts along dimension 1
There are 2 independent parts, one for each index of `groups`. A program takes and returns all parts, laid end to end along the dimension named above; each array names one. Nothing has to cross between parts.
Inputs may be any that keep to these rules, and one draw needn't show every extreme that they name: Each face's owner lies in the node range of its own partition or of a partition beside it, 4096 nodes a partition. `patch_count`: the first partition is full. `neighbours`: each neighbour differs from its patch by 1 to 4 in patch order.
All inputs are finite; a program needn't handle non-finite values.
Results may differ from a plain program's by a relative error of at most 0.0003.
Values may be sent and summed in bfloat16 or wider, within the bound.
A program may use at most 64 MiB of HBM per device.

v0:
```python
import functools

import jax
import jax.numpy as jnp
from jax import lax
from jax.experimental import pallas as pl
from jax.experimental.pallas import tpu as pltpu
from jax.sharding import PartitionSpec as P

NODES = 128
REACH = 4
SWEEPS = 4
LOW = 256
LANES = 128
SPLIT = 4
smoothing = 1.5
OFFSETS = [d for d in range(-REACH, REACH + 1) if d != 0]
NOFF = len(OFFSETS)
MESH = pl.DeviceIdType.MESH


def kernel(
    chunk,
    sens,
    owner,
    count,
    neighbours_in,
    coupling_in,
    surface_out,
    smooth_out,
    neighbours,
    coupling,
    link_sem,
    values,
    owners,
    masked,
    low_hot,
    acc,
    fields,
    weights,
    table,
    halo_out,
    halo_in,
    surface_stage,
    smooth_stage,
    out_sem,
    load_sem,
    oload_sem,
    send_sem,
    recv_sem,
    osend_sem,
    orecv_sem,
    hsend_sem,
    hrecv_sem,
):
    columns, faces = sens.shape
    patches = neighbours.shape[1]
    span = patches * NODES
    highs = span // LOW
    chunks = faces // chunk
    pieces = chunk // LANES
    orow = faces // LANES
    position = lax.axis_index("surf")
    peers = lax.axis_size("surf")
    has_below = position > 0
    has_above = position < peers - 1

    def local_load(k):
        return pltpu.make_async_copy(sens.at[:, pl.ds(k * chunk, chunk)], values.at[0, k], load_sem.at[k])

    def face_copy(side, k):
        target = position + 1 if side == 0 else position - 1
        return pltpu.make_async_remote_copy(
            src_ref=sens.at[:, pl.ds(k * chunk, chunk)],
            dst_ref=values.at[1 + side, k],
            send_sem=send_sem.at[side, k],
            recv_sem=recv_sem.at[side, k],
            device_id={"surf": target},
            device_id_type=MESH,
        )

    def owner_copy(side):
        target = position + 1 if side == 0 else position - 1
        return pltpu.make_async_remote_copy(
            src_ref=owner,
            dst_ref=owners.at[1 + side],
            send_sem=osend_sem.at[side],
            recv_sem=orecv_sem.at[side],
            device_id={"surf": target},
            device_id_type=MESH,
        )

    def halo_copy(side, sweep):
        target = position + 1 if side == 0 else position - 1
        if sweep == SWEEPS - 1:
            source = patches if side == 0 else REACH
            landing = 0 if side == 0 else patches + REACH
            src, dst = fields.at[sweep, pl.ds(source, REACH)], fields.at[sweep, pl.ds(landing, REACH)]
        else:
            src, dst = halo_out.at[side, sweep], halo_in.at[side, sweep]
        return pltpu.make_async_remote_copy(
            src_ref=src,
            dst_ref=dst,
            send_sem=hsend_sem.at[side, sweep],
            recv_sem=hrecv_sem.at[side, sweep],
            device_id={"surf": target},
            device_id_type=MESH,
        )

    own_owner = pltpu.make_async_copy(owner, owners.at[0], oload_sem)
    own_owner.start()
    link_copies = (
        pltpu.make_async_copy(neighbours_in, neighbours, link_sem.at[0]),
        pltpu.make_async_copy(coupling_in, coupling, link_sem.at[1]),
    )
    for link_copy in link_copies:
        link_copy.start()
    for k in range(chunks):
        local_load(k).start()

    barrier = pltpu.get_barrier_semaphore()

    @pl.when(has_below)
    def _():
        pl.semaphore_signal(barrier, inc=1, device_id={"surf": position - 1}, device_id_type=MESH)

    @pl.when(has_above)
    def _():
        pl.semaphore_signal(barrier, inc=1, device_id={"surf": position + 1}, device_id_type=MESH)

    both = jnp.logical_and(has_below, has_above)

    @pl.when(both)
    def _():
        pl.semaphore_wait(barrier, 2)

    @pl.when(jnp.logical_not(both))
    def _():
        pl.semaphore_wait(barrier, 1)

    @pl.when(has_above)
    def _():
        owner_copy(0).start()

    @pl.when(has_below)
    def _():
        owner_copy(1).start()

    for k in range(chunks):

        @pl.when(has_above)
        def _(k=k):
            face_copy(0, k).start()

        @pl.when(has_below)
        def _(k=k):
            face_copy(1, k).start()

    for link_copy in link_copies:
        link_copy.wait()
    slots = lax.broadcasted_iota(jnp.int32, neighbours.shape, 1)
    distance = neighbours[...] - (position * patches + slots)
    links = coupling[...]
    along = lax.broadcasted_iota(jnp.int32, (1, patches), 1)
    alive = jnp.where(along < count[0], 1.0, 0.0).astype(jnp.float32)
    share = alive / (1.0 + smoothing * (2.0 + jnp.sum(links, axis=0, keepdims=True)))
    lines = [
        smoothing * share * jnp.sum(jnp.where(distance == offset, links, 0.0), axis=0, keepdims=True)
        for offset in OFFSETS
    ]
    lines += [share, smoothing * share, alive]
    table[...] = jnp.zeros_like(table)
    for at, line in enumerate(lines):
        table[pl.ds(at, 1), pl.ds(0, patches)] = line
    turned = jnp.transpose(table[...])
    for at in range(len(lines)):
        weights[at] = jnp.broadcast_to(turned[0:patches, at : at + 1], (patches, LANES))

    zero_halo = jnp.zeros((REACH, columns, NODES), jnp.float32)

    @pl.when(jnp.logical_not(has_below))
    def _():
        for sweep in range(SWEEPS):
            fields[sweep, pl.ds(0, REACH)] = zero_halo

    @pl.when(jnp.logical_not(has_above))
    def _():
        for sweep in range(SWEEPS):
            fields[sweep, pl.ds(patches + REACH, REACH)] = zero_halo

    acc[...] = jnp.zeros_like(acc)
    first_node = position * span
    low_rows = lax.broadcasted_iota(jnp.int32, (LOW, LANES), 0)

    def add_chunk(slot, k):
        for j in range(pieces):
            local = owners[slot, pl.ds(k * pieces + j, 1), :] - first_node
            high = (local >> 8).astype(jnp.float32).astype(jnp.bfloat16)
            low = local & (LOW - 1)
            lanes = pl.ds(j * LANES, LANES)
            low_hot[:, lanes] = jnp.where(low_rows == low, 1.0, 0.0).astype(jnp.bfloat16)
            vals = values[slot, k, :, lanes]
            high_full = jnp.broadcast_to(high, vals.shape)
            for h in range(highs):
                masked[pl.ds(h * columns, columns), lanes] = jnp.where(
                    high_full == jnp.bfloat16(h), vals, jnp.bfloat16(0)
                )
        acc[...] += lax.dot_general(
            masked[...],
            low_hot[...],
            (((1,), (1,)), ((), ())),
            preferred_element_type=jnp.float32,
        )

    own_owner.wait()

    def step(s, carry):
        is_own = s < chunks
        t = jnp.maximum(s - chunks, 0)
        side = lax.rem(t, 2)
        k = jnp.where(is_own, s, t // 2)
        slot = jnp.where(is_own, 0, 1 + side)

        @pl.when(is_own)
        def _():
            local_load(k).wait()

        from_below = jnp.logical_and(jnp.logical_not(is_own), side == 0)
        from_above = jnp.logical_and(jnp.logical_not(is_own), side == 1)

        @pl.when(jnp.logical_and(from_below, has_below))
        def _():
            @pl.when(t == 0)
            def _():
                owner_copy(0).wait_recv()

            face_copy(0, k).wait_recv()

        @pl.when(jnp.logical_and(from_above, has_above))
        def _():
            @pl.when(t == 1)
            def _():
                owner_copy(1).wait_recv()

            face_copy(1, k).wait_recv()

        present = jnp.logical_or(
            is_own,
            jnp.logical_or(jnp.logical_and(side == 0, has_below), jnp.logical_and(side == 1, has_above)),
        )

        @pl.when(present)
        def _():
            add_chunk(slot, k)

        return carry

    lax.fori_loop(0, 3 * chunks, step, 0)

    def put_surface(h):
        for half in range(LOW // NODES):
            p = h * (LOW // NODES) + half
            patch = acc[pl.ds(h * columns, columns), pl.ds(half * NODES, NODES)]
            patch = patch * weights[NOFF + 2, pl.ds(p, 1), :]
            fields[0, REACH + p] = patch
            surface_stage[:, pl.ds(p * NODES, NODES)] = patch

    def send_halo(sweep):
        for side, there in ((0, has_above), (1, has_below)):

            @pl.when(there)
            def _(side=side):
                if sweep < SWEEPS - 1:
                    first = patches if side == 0 else REACH
                    halo_out[side, sweep] = fields[sweep, pl.ds(first, REACH)].astype(jnp.bfloat16)
                halo_copy(side, sweep).start()

    def wait_halo(sweep):
        for side, there in ((0, has_below), (1, has_above)):

            @pl.when(there)
            def _(side=side):
                halo_copy(side, sweep).wait_recv()
                if sweep < SWEEPS - 1:
                    first = 0 if side == 0 else patches + REACH
                    fields[sweep, pl.ds(first, REACH)] = halo_in[side, sweep].astype(jnp.float32)

    ends = REACH * NODES // LOW
    for h in list(range(ends)) + list(range(highs - ends, highs)):
        put_surface(h)
    send_halo(0)
    for h in range(ends, highs - ends):
        put_surface(h)

    surface_copy = pltpu.make_async_copy(surface_stage, surface_out, out_sem.at[0])
    surface_copy.start()

    def relax(sweep, p):
        parts = [weights[at, pl.ds(p, 1), :] for at in range(NOFF + 2)]
        for block in range(columns // 8):
            c = pl.ds(block * 8, 8)
            here = fields[sweep, p + REACH, c, :]
            total = parts[NOFF] * fields[0, p + REACH, c, :]
            total = total + parts[NOFF + 1] * (pltpu.roll(here, 1, 1) + pltpu.roll(here, NODES - 1, 1))
            for at, offset in enumerate(OFFSETS):
                total = total + parts[at] * fields[sweep, p + REACH + offset, c, :]
            if sweep == SWEEPS - 1:
                smooth_stage[c, pl.ds(pl.multiple_of(p * NODES, NODES), NODES)] = total
            else:
                fields[sweep + 1, p + REACH, c, :] = total

    def relax_range(sweep, low, high):
        def one(p, carry):
            relax(sweep, p)
            return carry

        lax.fori_loop(low, high, one, 0)

    for sweep in range(SWEEPS):
        last = sweep == SWEEPS - 1
        if last:
            relax_range(sweep, REACH, patches - REACH)
        wait_halo(sweep)
        relax_range(sweep, 0, REACH)
        relax_range(sweep, patches - REACH, patches)
        if not last:
            send_halo(sweep + 1)
            relax_range(sweep, REACH, patches - REACH)

    smooth_copy = pltpu.make_async_copy(smooth_stage, smooth_out, out_sem.at[1])
    smooth_copy.start()
    surface_copy.wait()
    smooth_copy.wait()

    for side, there in ((0, has_above), (1, has_below)):

        @pl.when(there)
        def _(side=side):
            owner_copy(side).wait_send()
            for k in range(chunks):
                face_copy(side, k).wait_send()
            for sweep in range(SWEEPS):
                halo_copy(side, sweep).wait_send()


def hand_over(surface, smooth, surface_out, smooth_out, stage, in_sem, out_sem):
    step = surface.shape[0] // SPLIT
    fetches, stores = [], []
    for at, (source, target) in enumerate(((surface, surface_out), (smooth, smooth_out))):
        for k in range(SPLIT):
            rows = pl.ds(k * step, step)
            fetches.append(pltpu.make_async_copy(source.at[rows], stage.at[at, rows], in_sem.at[at, k]))
            stores.append(pltpu.make_async_copy(stage.at[at, rows], target.at[rows], out_sem.at[at, k]))
    for fetch in fetches:
        fetch.start()
    for fetch, store in zip(fetches, stores):
        fetch.wait()
        store.start()
    for store in stores:
        store.wait()


def body(sensitivity, owner, patch_count, neighbours, coupling):
    columns, faces = sensitivity.shape
    patches = neighbours.shape[0]
    span = patches * NODES
    chunk = min(512, faces)
    chunks = faces // chunk
    highs = span // LOW
    hbm = pl.BlockSpec(memory_space=pltpu.HBM)
    vmem = pl.BlockSpec(memory_space=pltpu.VMEM)
    links = neighbours.T.shape
    out = jax.ShapeDtypeStruct((columns, span), jnp.float32)
    dma = pltpu.SemaphoreType.DMA
    outputs = pl.pallas_call(
        functools.partial(kernel, chunk),
        out_shape=(out, out),
        in_specs=[hbm, hbm, pl.BlockSpec(memory_space=pltpu.SMEM), hbm, hbm],
        out_specs=(hbm, hbm),
        scratch_shapes=[
            pltpu.VMEM(links, jnp.int32),
            pltpu.VMEM(links, jnp.float32),
            dma((2,)),
            pltpu.VMEM((3, chunks, columns, chunk), jnp.bfloat16),
            pltpu.VMEM((3, faces // LANES, LANES), jnp.int32),
            pltpu.VMEM((highs * columns, chunk), jnp.bfloat16),
            pltpu.VMEM((LOW, chunk), jnp.bfloat16),
            pltpu.VMEM((highs * columns, LOW), jnp.float32),
            pltpu.VMEM((SWEEPS, patches + 2 * REACH, columns, NODES), jnp.float32),
            pltpu.VMEM((NOFF + 3, patches, LANES), jnp.float32),
            pltpu.VMEM((16, LANES), jnp.float32),
            pltpu.VMEM((2, SWEEPS - 1, REACH, columns, NODES), jnp.bfloat16),
            pltpu.VMEM((2, SWEEPS - 1, REACH, columns, NODES), jnp.bfloat16),
            pltpu.VMEM((columns, span), jnp.float32),
            pltpu.VMEM((columns, span), jnp.float32),
            dma((2,)),
            dma((chunks,)),
            dma,
            dma((2, chunks)),
            dma((2, chunks)),
            dma((2,)),
            dma((2,)),
            dma((2, SWEEPS)),
            dma((2, SWEEPS)),
        ],
        compiler_params=pltpu.CompilerParams(
            collective_id=0, has_side_effects=True, vmem_limit_bytes=63 * 1024 * 1024
        ),
    )(sensitivity, owner.reshape(faces // LANES, LANES), patch_count, neighbours.T, coupling.T)
    return pl.pallas_call(
        hand_over,
        out_shape=(out, out),
        in_specs=[hbm, hbm],
        out_specs=(hbm, hbm),
        scratch_shapes=[pltpu.VMEM((2, columns, span), jnp.float32), dma((2, SPLIT)), dma((2, SPLIT))],
        compiler_params=pltpu.CompilerParams(vmem_limit_bytes=63 * 1024 * 1024),
    )(*outputs)


def solution(mesh):
    placed = (
        P(None, ("groups", "surf")),
        P(("groups", "surf")),
        P(("groups", "surf")),
        P(("groups", "surf"), None),
        P(("groups", "surf"), None),
    )
    return jax.shard_map(
        body,
        mesh=mesh,
        in_specs=placed,
        out_specs=(P(None, ("groups", "surf")), P(None, ("groups", "surf"))),
        check_vma=False,
    )
```

profile of v0, /device:TPU:1, one launch (start us, length us, event | category | flops | bytes accessed | tf_op | source)
XLA Modules:
  0.0 49.5 jit_solution(2022621437485439089)
XLA Ops:
  1.3 45.4 %shard_map.68 = (f32[96,4096]{1,0:T(8,128)}, f32[96,4096]{1,0:T(8,128)}) custom-call(bf16[96,4096]{1,0:T(8,128)(2,1)} %sens.1, s32[32,128]{1,0:T(8,128)} %bitcast.3, s32[1]{0:T(128)S(6)} %copy.7.count, s32[9,32]{1,0:T(8,128)} %bitcast.4, f32[9,32]{1,0:T(8,128)} %bitcast.5), custom_call_target="tpu_custom_call" | custom-call | tf_op jit(solution)/shard_map/pallas_call | solution.py:375
  46.7 2.8 %shard_map.69 = (f32[96,4096]{1,0:T(8,128)}, f32[96,4096]{1,0:T(8,128)}) custom-call(f32[96,4096]{1,0:T(8,128)} %get-tuple-element.4.surface, f32[96,4096]{1,0:T(8,128)} %get-tuple-element.5.smooth), custom_call_target="tpu_custom_call" | custom-call | tf_op jit(solution)/shard_map/pallas_call | solution.py:410
where the time goes:
time: 49.6 us; the launch traced here: 49.5 us
  Pallas kernels  48.2 us (97%)
  between operations  1.28 us (3%)
    pallas_call x1, Pallas kernels, body(): pl.pallas_call(functools.partial(kernel, chunk), out_shape=(out, out), in...  45.4 us
    pallas_call x1, Pallas kernels, body(): pl.pallas_call(hand_over, out_shape=(out, out), in_specs=[hbm, hbm], out_...  2.79 us

commit v1 on v0

--- a/solution.py
+++ b/solution.py
@@ -12,7 +12,8 @@
 SWEEPS = 4
 LOW = 256
 LANES = 128
-SPLIT = 4
+PAIR = 2
+BATCH = 8
 smoothing = 1.5
 OFFSETS = [d for d in range(-REACH, REACH + 1) if d != 0]
 NOFF = len(OFFSETS)
@@ -26,8 +27,8 @@
     count,
     neighbours_in,
     coupling_in,
-    surface_out,
-    smooth_out,
+    surface_stage,
+    smooth_stage,
     neighbours,
     coupling,
     link_sem,
@@ -41,8 +42,6 @@
     table,
     halo_out,
     halo_in,
-    surface_stage,
-    smooth_stage,
     out_sem,
     load_sem,
     oload_sem,
@@ -174,7 +173,8 @@
         table[pl.ds(at, 1), pl.ds(0, patches)] = line
     turned = jnp.transpose(table[...])
     for at in range(len(lines)):
-        weights[at] = jnp.broadcast_to(turned[0:patches, at : at + 1], (patches, LANES))
+        line = jnp.broadcast_to(turned[0:patches, at : at + 1], (patches, LANES))
+        weights[at] = jnp.broadcast_to(line[:, None, :], (patches, 8, LANES))
 
     zero_halo = jnp.zeros((REACH, columns, NODES), jnp.float32)
 
@@ -261,7 +261,7 @@
         for half in range(LOW // NODES):
             p = h * (LOW // NODES) + half
             patch = acc[pl.ds(h * columns, columns), pl.ds(half * NODES, NODES)]
-            patch = patch * weights[NOFF + 2, pl.ds(p, 1), :]
+            patch = patch * weights[NOFF + 2, p, 0:1, :]
             fields[0, REACH + p] = patch
             surface_stage[:, pl.ds(p * NODES, NODES)] = patch
 
@@ -292,45 +292,44 @@
     for h in range(ends, highs - ends):
         put_surface(h)
 
-    surface_copy = pltpu.make_async_copy(surface_stage, surface_out, out_sem.at[0])
-    surface_copy.start()
-
-    def relax(sweep, p):
-        parts = [weights[at, pl.ds(p, 1), :] for at in range(NOFF + 2)]
-        for block in range(columns // 8):
-            c = pl.ds(block * 8, 8)
-            here = fields[sweep, p + REACH, c, :]
-            total = parts[NOFF] * fields[0, p + REACH, c, :]
-            total = total + parts[NOFF + 1] * (pltpu.roll(here, 1, 1) + pltpu.roll(here, NODES - 1, 1))
-            for at, offset in enumerate(OFFSETS):
-                total = total + parts[at] * fields[sweep, p + REACH + offset, c, :]
-            if sweep == SWEEPS - 1:
-                smooth_stage[c, pl.ds(pl.multiple_of(p * NODES, NODES), NODES)] = total
-            else:
-                fields[sweep + 1, p + REACH, c, :] = total
-
-    def relax_range(sweep, low, high):
-        def one(p, carry):
-            relax(sweep, p)
+
+    def relax(sweep, first, count):
+        for group in range(0, columns, 8 * PAIR):
+            blocks = [pl.ds(group + 8 * k, 8) for k in range(PAIR)]
+            window = [[fields[sweep, first + q, c, :] for q in range(2 * REACH)] for c in blocks]
+            for at in range(count):
+                p = first + at
+                parts = [weights[line, p] for line in range(NOFF + 2)]
+                for k, c in enumerate(blocks):
+                    window[k].append(fields[sweep, p + 2 * REACH, c, :])
+                    here = window[k][at + REACH]
+                    terms = [parts[line] * window[k][at + REACH + offset] for line, offset in enumerate(OFFSETS)]
+                    terms.append(parts[NOFF] * fields[0, p + REACH, c, :])
+                    terms.append(parts[NOFF + 1] * (pltpu.roll(here, 1, 1) + pltpu.roll(here, NODES - 1, 1)))
+                    while len(terms) > 1:
+                        terms = [sum(terms[n : n + 2][1:], terms[n]) for n in range(0, len(terms), 2)]
+                    if sweep == SWEEPS - 1:
+                        smooth_stage[c, pl.ds(pl.multiple_of(p * NODES, NODES), NODES)] = terms[0]
+                    else:
+                        fields[sweep + 1, p + REACH, c, :] = terms[0]
+
+    def relax_inner(sweep):
+        def one(step, carry):
+            relax(sweep, REACH + step * BATCH, BATCH)
             return carry
 
-        lax.fori_loop(low, high, one, 0)
+        lax.fori_loop(0, (patches - 2 * REACH) // BATCH, one, 0)
 
     for sweep in range(SWEEPS):
         last = sweep == SWEEPS - 1
         if last:
-            relax_range(sweep, REACH, patches - REACH)
+            relax_inner(sweep)
         wait_halo(sweep)
-        relax_range(sweep, 0, REACH)
-        relax_range(sweep, patches - REACH, patches)
+        relax(sweep, 0, REACH)
+        relax(sweep, patches - REACH, REACH)
         if not last:
             send_halo(sweep + 1)
-            relax_range(sweep, REACH, patches - REACH)
-
-    smooth_copy = pltpu.make_async_copy(smooth_stage, smooth_out, out_sem.at[1])
-    smooth_copy.start()
-    surface_copy.wait()
-    smooth_copy.wait()
+            relax_inner(sweep)
 
     for side, there in ((0, has_above), (1, has_below)):
 
@@ -343,21 +342,15 @@
                 halo_copy(side, sweep).wait_send()
 
 
-def hand_over(surface, smooth, surface_out, smooth_out, stage, in_sem, out_sem):
-    step = surface.shape[0] // SPLIT
-    fetches, stores = [], []
-    for at, (source, target) in enumerate(((surface, surface_out), (smooth, smooth_out))):
-        for k in range(SPLIT):
-            rows = pl.ds(k * step, step)
-            fetches.append(pltpu.make_async_copy(source.at[rows], stage.at[at, rows], in_sem.at[at, k]))
-            stores.append(pltpu.make_async_copy(stage.at[at, rows], target.at[rows], out_sem.at[at, k]))
-    for fetch in fetches:
-        fetch.start()
-    for fetch, store in zip(fetches, stores):
-        fetch.wait()
-        store.start()
-    for store in stores:
-        store.wait()
+def hand_over(surface, smooth, surface_out, smooth_out, out_sem):
+    copies = [
+        pltpu.make_async_copy(surface, surface_out, out_sem.at[0]),
+        pltpu.make_async_copy(smooth, smooth_out, out_sem.at[1]),
+    ]
+    for copy in copies:
+        copy.start()
+    for copy in copies:
+        copy.wait()
 
 
 def body(sensitivity, owner, patch_count, neighbours, coupling):
@@ -374,9 +367,9 @@
     dma = pltpu.SemaphoreType.DMA
     outputs = pl.pallas_call(
         functools.partial(kernel, chunk),
-        out_shape=(out, out),
+        out_shape=(pltpu.VMEM((columns, span), jnp.float32),) * 2,
         in_specs=[hbm, hbm, pl.BlockSpec(memory_space=pltpu.SMEM), hbm, hbm],
-        out_specs=(hbm, hbm),
+        out_specs=(vmem, vmem),
         scratch_shapes=[
             pltpu.VMEM(links, jnp.int32),
             pltpu.VMEM(links, jnp.float32),
@@ -387,12 +380,10 @@
             pltpu.VMEM((LOW, chunk), jnp.bfloat16),
             pltpu.VMEM((highs * columns, LOW), jnp.float32),
             pltpu.VMEM((SWEEPS, patches + 2 * REACH, columns, NODES), jnp.float32),
-            pltpu.VMEM((NOFF + 3, patches, LANES), jnp.float32),
+            pltpu.VMEM((NOFF + 3, patches, 8, LANES), jnp.float32),
             pltpu.VMEM((16, LANES), jnp.float32),
             pltpu.VMEM((2, SWEEPS - 1, REACH, columns, NODES), jnp.bfloat16),
             pltpu.VMEM((2, SWEEPS - 1, REACH, columns, NODES), jnp.bfloat16),
-            pltpu.VMEM((columns, span), jnp.float32),
-            pltpu.VMEM((columns, span), jnp.float32),
             dma((2,)),
             dma((chunks,)),
             dma,
@@ -404,16 +395,16 @@
             dma((2, SWEEPS)),
         ],
         compiler_params=pltpu.CompilerParams(
-            collective_id=0, has_side_effects=True, vmem_limit_bytes=63 * 1024 * 1024
+            collective_id=0, has_side_effects=True, vmem_limit_bytes=60 * 1024 * 1024
         ),
     )(sensitivity, owner.reshape(faces // LANES, LANES), patch_count, neighbours.T, coupling.T)
     return pl.pallas_call(
         hand_over,
         out_shape=(out, out),
-        in_specs=[hbm, hbm],
+        in_specs=[vmem, vmem],
         out_specs=(hbm, hbm),
-        scratch_shapes=[pltpu.VMEM((2, columns, span), jnp.float32), dma((2, SPLIT)), dma((2, SPLIT))],
-        compiler_params=pltpu.CompilerParams(vmem_limit_bytes=63 * 1024 * 1024),
+        scratch_shapes=[dma((2,))],
+        compiler_params=pltpu.CompilerParams(vmem_limit_bytes=16 * 1024 * 1024),
     )(*outputs)
 
 

time: 49.6 us -> 45.3 us (0.913)
  the two profiles are of different devices: /device:TPU:1 before, /device:TPU:11 now
where the time goes in v1:
time: 45.3 us; the launch traced here: 44.5 us
  Pallas kernels  43.2 us (95%)
  between operations  1.28 us (3%)
    pallas_call x1, Pallas kernels, body(): pl.pallas_call(functools.partial(kernel, chunk), out_shape=(pltpu.VMEM((c...  41.5 us
    pallas_call x1, Pallas kernels, body(): pl.pallas_call(hand_over, out_shape=(out, out), in_specs=[vmem, vmem], ou...  1.68 us

profile of v1, /device:TPU:11, one launch (start us, length us, event | category | flops | bytes accessed | tf_op | source)
XLA Modules:
  0.0 44.5 jit_solution(10515171180846393946)
XLA Ops:
  1.3 41.5 %shard_map.68 = (f32[96,4096]{1,0:T(8,128)S(1)}, f32[96,4096]{1,0:T(8,128)S(1)}) custom-call(bf16[96,4096]{1,0:T(8,128)(2,1)} %sens.1, s32[32,128]{1,0:T(8,128)} %bitcast.3, s32[1]{0:T(128)S(6)} %copy.7.count, s32[9,32]{1,0:T(8,128)} %bitcast.4, f32[9,32]{1,0:T(8,128)} %bitcast.5), custom_call_target="tpu_custom_call" | custom-call | tf_op jit(solution)/shard_map/pallas_call | solution.py:368
  42.8 1.7 %shard_map.69 = (f32[96,4096]{1,0:T(8,128)}, f32[96,4096]{1,0:T(8,128)}) custom-call(f32[96,4096]{1,0:T(8,128)S(1)} %get-tuple-element.4.surface, f32[96,4096]{1,0:T(8,128)S(1)} %get-tuple-element.5.smooth), custom_call_target="tpu_custom_call" | custom-call | tf_op jit(solution)/shard_map/pallas_call | solution.py:401

commit v2 on v1

v2 whole, which is shorter than its diff:
```python
import functools

import jax
import jax.numpy as jnp
from jax import lax
from jax.experimental import pallas as pl
from jax.experimental.pallas import tpu as pltpu
from jax.sharding import PartitionSpec as P

NODES = 128
REACH = 4
SWEEPS = 4
LOW = 256
LANES = 128
PAIR = 2
BATCH = 8
BLOCK = 512
SLOTS = 256
WIDE = 1024
VMEM_LIMIT = 60 * 1024 * 1024
smoothing = 1.5
OFFSETS = [d for d in range(-REACH, REACH + 1) if d != 0]
NOFF = len(OFFSETS)
MESH = pl.DeviceIdType.MESH


def prepare(count, neighbours, coupling, table, weights, fields):
    patches, columns = neighbours.shape[1], fields.shape[2]
    position = lax.axis_index("surf")
    has_below = position > 0
    has_above = position < lax.axis_size("surf") - 1
    slots = lax.broadcasted_iota(jnp.int32, neighbours.shape, 1)
    distance = neighbours[...] - (position * patches + slots)
    links = coupling[...]
    along = lax.broadcasted_iota(jnp.int32, (1, patches), 1)
    alive = jnp.where(along < count[0], 1.0, 0.0).astype(jnp.float32)
    share = alive / (1.0 + smoothing * (2.0 + jnp.sum(links, axis=0, keepdims=True)))
    lines = [
        smoothing * share * jnp.sum(jnp.where(distance == offset, links, 0.0), axis=0, keepdims=True)
        for offset in OFFSETS
    ]
    lines += [share, smoothing * share, alive]
    table[...] = jnp.zeros_like(table)
    for at, line in enumerate(lines):
        table[pl.ds(at, 1), pl.ds(0, patches)] = line
    turned = jnp.transpose(table[...])
    for at in range(len(lines)):
        line = jnp.broadcast_to(turned[0:patches, at : at + 1], (patches, LANES))
        weights[at] = jnp.broadcast_to(line[:, None, :], (patches, 8, LANES))

    zero_halo = jnp.zeros((REACH, columns, NODES), jnp.float32)

    @pl.when(jnp.logical_not(has_below))
    def _():
        for sweep in range(SWEEPS):
            fields[sweep, pl.ds(0, REACH)] = zero_halo

    @pl.when(jnp.logical_not(has_above))
    def _():
        for sweep in range(SWEEPS):
            fields[sweep, pl.ds(patches + REACH, REACH)] = zero_halo


def relaxation(acc, fields, weights, halo_out, halo_in, hsend_sem, hrecv_sem, surface_stage, smooth_stage, aside):
    columns = fields.shape[2]
    patches = fields.shape[1] - 2 * REACH
    highs = patches * NODES // LOW
    position = lax.axis_index("surf")
    has_below = position > 0
    has_above = position < lax.axis_size("surf") - 1

    def halo_copy(side, sweep):
        target = position + 1 if side == 0 else position - 1
        if sweep == SWEEPS - 1:
            source = patches if side == 0 else REACH
            landing = 0 if side == 0 else patches + REACH
            src, dst = fields.at[sweep, pl.ds(source, REACH)], fields.at[sweep, pl.ds(landing, REACH)]
        else:
            src, dst = halo_out.at[side, sweep], halo_in.at[side, sweep]
        return pltpu.make_async_remote_copy(
            src_ref=src,
            dst_ref=dst,
            send_sem=hsend_sem.at[side, sweep],
            recv_sem=hrecv_sem.at[side, sweep],
            device_id={"surf": target},
            device_id_type=MESH,
        )

    def put_surface(h):
        for half in range(LOW // NODES):
            p = h * (LOW // NODES) + half
            patch = acc[pl.ds(h * columns, columns), pl.ds(half * NODES, NODES)]
            patch = patch * weights[NOFF + 2, p, 0:1, :]
            fields[0, REACH + p] = patch
            surface_stage[:, pl.ds(p * NODES, NODES)] = patch

    def send_halo(sweep):
        for side, there in ((0, has_above), (1, has_below)):

            @pl.when(there)
            def _(side=side):
                if sweep < SWEEPS - 1:
                    first = patches if side == 0 else REACH
                    halo_out[side, sweep] = fields[sweep, pl.ds(first, REACH)].astype(jnp.bfloat16)
                halo_copy(side, sweep).start()

    def wait_halo(sweep):
        for side, there in ((0, has_below), (1, has_above)):

            @pl.when(there)
            def _(side=side):
                halo_copy(side, sweep).wait_recv()
                if sweep < SWEEPS - 1:
                    first = 0 if side == 0 else patches + REACH
                    fields[sweep, pl.ds(first, REACH)] = halo_in[side, sweep].astype(jnp.float32)

    ends = REACH * NODES // LOW
    for h in list(range(ends)) + list(range(highs - ends, highs)):
        put_surface(h)
    send_halo(0)
    for h in range(ends, highs - ends):
        put_surface(h)


    def relax(sweep, first, count):
        for group in range(0, columns, 8 * PAIR):
            blocks = [pl.ds(group + 8 * k, 8) for k in range(PAIR)]
            window = [[fields[sweep, first + q, c, :] for q in range(2 * REACH)] for c in blocks]
            for at in range(count):
                p = first + at
                parts = [weights[line, p] for line in range(NOFF + 2)]
                for k, c in enumerate(blocks):
                    window[k].append(fields[sweep, p + 2 * REACH, c, :])
                    here = window[k][at + REACH]
                    terms = [parts[line] * window[k][at + REACH + offset] for line, offset in enumerate(OFFSETS)]
                    terms.append(parts[NOFF] * fields[0, p + REACH, c, :])
                    terms.append(parts[NOFF + 1] * (pltpu.roll(here, 1, 1) + pltpu.roll(here, NODES - 1, 1)))
                    while len(terms) > 1:
                        terms = [sum(terms[n : n + 2][1:], terms[n]) for n in range(0, len(terms), 2)]
                    if sweep == SWEEPS - 1:
                        smooth_stage[c, pl.ds(pl.multiple_of(p * NODES, NODES), NODES)] = terms[0]
                    else:
                        fields[sweep + 1, p + REACH, c, :] = terms[0]

    def relax_inner(sweep):
        def one(step, carry):
            relax(sweep, REACH + step * BATCH, BATCH)
            return carry

        lax.fori_loop(0, (patches - 2 * REACH) // BATCH, one, 0)

    for sweep in range(SWEEPS):
        last = sweep == SWEEPS - 1
        if last:
            relax_inner(sweep)
        aside(sweep)
        wait_halo(sweep)
        relax(sweep, 0, REACH)
        relax(sweep, patches - REACH, REACH)
        if not last:
            send_halo(sweep + 1)
            relax_inner(sweep)

    for side, there in ((0, has_above), (1, has_below)):

        @pl.when(there)
        def _(side=side):
            for sweep in range(SWEEPS):
                halo_copy(side, sweep).wait_send()


def kernel(
    chunk,
    sens,
    owner,
    count,
    neighbours_in,
    coupling_in,
    surface_stage,
    smooth_stage,
    neighbours,
    coupling,
    link_sem,
    values,
    owners,
    masked,
    low_hot,
    acc,
    fields,
    weights,
    table,
    halo_out,
    halo_in,
    out_sem,
    load_sem,
    oload_sem,
    send_sem,
    recv_sem,
    osend_sem,
    orecv_sem,
    hsend_sem,
    hrecv_sem,
):
    columns, faces = sens.shape
    patches = neighbours.shape[1]
    span = patches * NODES
    highs = span // LOW
    chunks = faces // chunk
    pieces = chunk // LANES
    orow = faces // LANES
    position = lax.axis_index("surf")
    peers = lax.axis_size("surf")
    has_below = position > 0
    has_above = position < peers - 1

    def local_load(k):
        return pltpu.make_async_copy(sens.at[:, pl.ds(k * chunk, chunk)], values.at[0, k], load_sem.at[k])

    def face_copy(side, k):
        target = position + 1 if side == 0 else position - 1
        return pltpu.make_async_remote_copy(
            src_ref=sens.at[:, pl.ds(k * chunk, chunk)],
            dst_ref=values.at[1 + side, k],
            send_sem=send_sem.at[side, k],
            recv_sem=recv_sem.at[side, k],
            device_id={"surf": target},
            device_id_type=MESH,
        )

    def owner_copy(side):
        target = position + 1 if side == 0 else position - 1
        return pltpu.make_async_remote_copy(
            src_ref=owner,
            dst_ref=owners.at[1 + side],
            send_sem=osend_sem.at[side],
            recv_sem=orecv_sem.at[side],
            device_id={"surf": target},
            device_id_type=MESH,
        )

    own_owner = pltpu.make_async_copy(owner, owners.at[0], oload_sem)
    own_owner.start()
    link_copies = (
        pltpu.make_async_copy(neighbours_in, neighbours, link_sem.at[0]),
        pltpu.make_async_copy(coupling_in, coupling, link_sem.at[1]),
    )
    for link_copy in link_copies:
        link_copy.start()
    for k in range(chunks):
        local_load(k).start()

    barrier = pltpu.get_barrier_semaphore()

    @pl.when(has_below)
    def _():
        pl.semaphore_signal(barrier, inc=1, device_id={"surf": position - 1}, device_id_type=MESH)

    @pl.when(has_above)
    def _():
        pl.semaphore_signal(barrier, inc=1, device_id={"surf": position + 1}, device_id_type=MESH)

    both = jnp.logical_and(has_below, has_above)

    @pl.when(both)
    def _():
        pl.semaphore_wait(barrier, 2)

    @pl.when(jnp.logical_not(both))
    def _():
        pl.semaphore_wait(barrier, 1)

    @pl.when(has_above)
    def _():
        owner_copy(0).start()

    @pl.when(has_below)
    def _():
        owner_copy(1).start()

    for k in range(chunks):

        @pl.when(has_above)
        def _(k=k):
            face_copy(0, k).start()

        @pl.when(has_below)
        def _(k=k):
            face_copy(1, k).start()

    for link_copy in link_copies:
        link_copy.wait()
    prepare(count, neighbours, coupling, table, weights, fields)

    acc[...] = jnp.zeros_like(acc)
    first_node = position * span
    low_rows = lax.broadcasted_iota(jnp.int32, (LOW, LANES), 0)

    def add_chunk(slot, k):
        for j in range(pieces):
            local = owners[slot, pl.ds(k * pieces + j, 1), :] - first_node
            high = (local >> 8).astype(jnp.float32).astype(jnp.bfloat16)
            low = local & (LOW - 1)
            lanes = pl.ds(j * LANES, LANES)
            low_hot[:, lanes] = jnp.where(low_rows == low, 1.0, 0.0).astype(jnp.bfloat16)
            vals = values[slot, k, :, lanes]
            high_full = jnp.broadcast_to(high, vals.shape)
            for h in range(highs):
                masked[pl.ds(h * columns, columns), lanes] = jnp.where(
                    high_full == jnp.bfloat16(h), vals, jnp.bfloat16(0)
                )
        acc[...] += lax.dot_general(
            masked[...],
            low_hot[...],
            (((1,), (1,)), ((), ())),
            preferred_element_type=jnp.float32,
        )

    own_owner.wait()

    def step(s, carry):
        is_own = s < chunks
        t = jnp.maximum(s - chunks, 0)
        side = lax.rem(t, 2)
        k = jnp.where(is_own, s, t // 2)
        slot = jnp.where(is_own, 0, 1 + side)

        @pl.when(is_own)
        def _():
            local_load(k).wait()

        from_below = jnp.logical_and(jnp.logical_not(is_own), side == 0)
        from_above = jnp.logical_and(jnp.logical_not(is_own), side == 1)

        @pl.when(jnp.logical_and(from_below, has_below))
        def _():
            @pl.when(t == 0)
            def _():
                owner_copy(0).wait_recv()

            face_copy(0, k).wait_recv()

        @pl.when(jnp.logical_and(from_above, has_above))
        def _():
            @pl.when(t == 1)
            def _():
                owner_copy(1).wait_recv()

            face_copy(1, k).wait_recv()

        present = jnp.logical_or(
            is_own,
            jnp.logical_or(jnp.logical_and(side == 0, has_below), jnp.logical_and(side == 1, has_above)),
        )

        @pl.when(present)
        def _():
            add_chunk(slot, k)

        return carry

    lax.fori_loop(0, 3 * chunks, step, 0)

    relaxation(
        acc, fields, weights, halo_out, halo_in, hsend_sem, hrecv_sem, surface_stage, smooth_stage, lambda sweep: None
    )

    for side, there in ((0, has_above), (1, has_below)):

        @pl.when(there)
        def _(side=side):
            owner_copy(side).wait_send()
            for k in range(chunks):
                face_copy(side, k).wait_send()


def packed_kernel(
    sens,
    owner,
    count,
    neighbours_in,
    coupling_in,
    surface_stage,
    smooth_stage,
    full_out,
    neighbours,
    coupling,
    link_sem,
    values,
    owners,
    nodes,
    spots,
    values_out,
    nodes_out,
    sort_hot,
    masked,
    low_hot,
    acc,
    fields,
    weights,
    table,
    halo_out,
    halo_in,
    flags,
    flags_in,
    load_sem,
    oload_sem,
    send_sem,
    recv_sem,
    nsend_sem,
    nrecv_sem,
    hsend_sem,
    hrecv_sem,
    fsend_sem,
    frecv_sem,
):
    columns, faces = sens.shape
    patches = neighbours.shape[1]
    span = patches * NODES
    highs = span // LOW
    rows = faces // LANES
    owns = faces // WIDE
    blocks = faces // BLOCK
    pieces = WIDE // LANES
    fit = WIDE // SLOTS
    others = blocks // fit
    position = lax.axis_index("surf")
    peers = lax.axis_size("surf")
    rounds = peers.bit_length() - 1
    has_below = position > 0
    has_above = position < peers - 1
    first_node = position * span

    def partner(step):
        size = 2 ** step
        return position + size - 2 * size * (lax.div(position, size) % 2)

    def local_load(k):
        return pltpu.make_async_copy(sens.at[:, pl.ds(k * WIDE, WIDE)], values.at[k], load_sem.at[k])

    def value_copy(side, k, q):
        target = position + 1 if side == 0 else position - 1
        lanes = pl.ds(pl.multiple_of(q * SLOTS, SLOTS), SLOTS)
        return pltpu.make_async_remote_copy(
            src_ref=values_out.at[side, k, :, lanes],
            dst_ref=values.at[owns + 2 * k + side, :, lanes],
            send_sem=send_sem.at[side, k, q],
            recv_sem=recv_sem.at[side, k, q],
            device_id={"surf": target},
            device_id_type=MESH,
        )

    def node_copy(side, k):
        target = position + 1 if side == 0 else position - 1
        return pltpu.make_async_remote_copy(
            src_ref=nodes_out.at[side, k],
            dst_ref=nodes.at[owns + 2 * k + side],
            send_sem=nsend_sem.at[side, k],
            recv_sem=nrecv_sem.at[side, k],
            device_id={"surf": target},
            device_id_type=MESH,
        )

    def flag_copy(step):
        return pltpu.make_async_remote_copy(
            src_ref=flags.at[step],
            dst_ref=flags_in.at[step],
            send_sem=fsend_sem.at[step],
            recv_sem=frecv_sem.at[step],
            device_id={"surf": partner(step)},
            device_id_type=MESH,
        )

    own_owner = pltpu.make_async_copy(owner, owners, oload_sem)
    own_owner.start()
    for k in range(owns):
        local_load(k).start()
    link_copies = (
        pltpu.make_async_copy(neighbours_in, neighbours, link_sem.at[0]),
        pltpu.make_async_copy(coupling_in, coupling, link_sem.at[1]),
    )
    for link_copy in link_copies:
        link_copy.start()

    barrier = pltpu.get_barrier_semaphore()

    @pl.when(has_below)
    def _():
        pl.semaphore_signal(barrier, inc=1, device_id={"surf": position - 1}, device_id_type=MESH)

    @pl.when(has_above)
    def _():
        pl.semaphore_signal(barrier, inc=1, device_id={"surf": position + 1}, device_id_type=MESH)

    for step in range(rounds):
        pl.semaphore_signal(barrier, inc=1, device_id={"surf": partner(step)}, device_id_type=MESH)

    own_owner.wait()
    local = owners[...] - first_node
    for k in range(owns):
        nodes[k] = local[k * pieces : (k + 1) * pieces]
    leaves = jnp.concatenate([local - (span - 1), -local], axis=0) > 0
    marks = jnp.where(leaves, 1.0, 0.0).astype(jnp.bfloat16)
    down = lax.broadcasted_iota(jnp.int32, (LANES, LANES), 0)
    along = lax.broadcasted_iota(jnp.int32, (LANES, LANES), 1)
    earlier = jnp.where(down < along, 1.0, 0.0).astype(jnp.bfloat16)
    block_rows = BLOCK // LANES
    down = lax.broadcasted_iota(jnp.int32, (2 * rows, 2 * rows), 0)
    along = lax.broadcasted_iota(jnp.int32, (2 * rows, 2 * rows), 1)
    same = lax.div(down, block_rows) == lax.div(along, block_rows)
    above = jnp.where(same & (along < down), 1.0, 0.0).astype(jnp.bfloat16)
    sums = jnp.dot(marks, jnp.ones((LANES, LANES), jnp.bfloat16), preferred_element_type=jnp.float32)
    place = jnp.dot(marks, earlier, preferred_element_type=jnp.float32)
    place += jnp.dot(above, sums.astype(jnp.bfloat16), preferred_element_type=jnp.float32)
    spots[...] = jnp.where(leaves, place, 2.0 * SLOTS)
    over = jnp.where(leaves & (place > SLOTS - 0.5), 1.0, 0.0)
    flags[0] = functools.reduce(jnp.maximum, [over[8 * n : 8 * n + 8] for n in range(2 * rows // 8)])

    both = jnp.logical_and(has_below, has_above)

    @pl.when(both)
    def _():
        pl.semaphore_wait(barrier, 2 + rounds)

    @pl.when(jnp.logical_not(both))
    def _():
        pl.semaphore_wait(barrier, 1 + rounds)

    flag_copy(0).start()
    for k in range(owns):
        local_load(k).wait()

    slot_rows = lax.broadcasted_iota(jnp.int32, (SLOTS, LANES), 0).astype(jnp.float32).astype(jnp.bfloat16)
    code_rows = lax.broadcasted_iota(jnp.int32, (16, LANES), 0)
    in_wide = WIDE // BLOCK

    def pack(k, carry):
        for q in range(fit):
            at = k * fit + q
            codes = []
            for j in range(block_rows):
                lanes = pl.ds(j * LANES, LANES)
                row = at * block_rows + j
                node = owners[pl.ds(row, 1), :]
                high = jnp.broadcast_to((node >> 8) & (highs - 1), (16, LANES))
                low = jnp.broadcast_to(node & (LOW - 1), (16, LANES))
                code = jnp.where(code_rows == 0, high, jnp.where(code_rows == 1, low, 0))
                codes.append(code.astype(jnp.float32).astype(jnp.bfloat16))
                for side in range(2):
                    spot = spots[pl.ds(side * rows + row, 1), :].astype(jnp.bfloat16)
                    spot = jnp.broadcast_to(spot, (SLOTS, LANES))
                    sort_hot[q % 2, pl.ds(side * SLOTS, SLOTS), lanes] = jnp.where(
                        spot == slot_rows, jnp.bfloat16(1), jnp.bfloat16(0)
                    )
            own = values[k * (fit // in_wide) + q // in_wide, :, pl.ds((q % in_wide) * BLOCK, BLOCK)]
            left = jnp.concatenate([own, jnp.concatenate(codes, axis=1)], axis=0)
            moved = lax.dot_general(
                left, sort_hot[q % 2], (((1,), (1,)), ((), ())), preferred_element_type=jnp.float32
            )
            node = (moved[columns : columns + 1] * LOW + moved[columns + 1 : columns + 2]).astype(jnp.int32)
            for side, there in ((0, has_above), (1, has_below)):
                values_out[side, k, :, pl.ds(q * SLOTS, SLOTS)] = moved[
                    0:columns, side * SLOTS : (side + 1) * SLOTS
                ].astype(jnp.bfloat16)
                for j in range(SLOTS // LANES):
                    nodes_out[side, k, pl.ds(q * (SLOTS // LANES) + j, 1), :] = node[
                        :, side * SLOTS + j * LANES : side * SLOTS + (j + 1) * LANES
                    ]

                @pl.when(there)
                def _(side=side, q=q):
                    value_copy(side, k, q).start()

        for side, there in ((0, has_above), (1, has_below)):

            @pl.when(there)
            def _(side=side):
                node_copy(side, k).start()

        return carry

    lax.fori_loop(0, others, pack, 0)

    for link_copy in link_copies:
        link_copy.wait()
    prepare(count, neighbours, coupling, table, weights, fields)
    acc[...] = jnp.zeros_like(acc)

    def add_chunk(s):
        for j in range(pieces):
            node = nodes[s, pl.ds(j, 1), :]
            high = (node >> 8).astype(jnp.float32).astype(jnp.bfloat16)
            low = (node & (LOW - 1)).astype(jnp.float32).astype(jnp.bfloat16)
            lanes = pl.ds(j * LANES, LANES)
            low_hot[:, lanes] = jnp.where(
                slot_rows == jnp.broadcast_to(low, (LOW, LANES)), jnp.bfloat16(1), jnp.bfloat16(0)
            )
            vals = values[s, :, lanes]
            high_full = jnp.broadcast_to(high, vals.shape)
            for h in range(highs):
                masked[pl.ds(h * columns, columns), lanes] = jnp.where(
                    high_full == jnp.bfloat16(h), vals, jnp.bfloat16(0)
                )
        acc[...] += lax.dot_general(
            masked[...], low_hot[...], (((1,), (1,)), ((), ())), preferred_element_type=jnp.float32
        )

    def step(s, carry):
        t = jnp.maximum(s - owns, 0)
        side = lax.rem(t, 2)
        k = lax.div(t, 2)
        is_own = s < owns
        from_below = jnp.logical_and(jnp.logical_not(is_own), jnp.logical_and(side == 0, has_below))
        from_above = jnp.logical_and(jnp.logical_not(is_own), jnp.logical_and(side == 1, has_above))

        @pl.when(from_below)
        def _():
            node_copy(0, k).wait_recv()
            for q in range(fit):
                value_copy(0, k, q).wait_recv()

        @pl.when(from_above)
        def _():
            node_copy(1, k).wait_recv()
            for q in range(fit):
                value_copy(1, k, q).wait_recv()

        @pl.when(jnp.logical_or(is_own, jnp.logical_or(from_below, from_above)))
        def _():
            add_chunk(s)

        return carry

    lax.fori_loop(0, owns + 2 * others, step, 0)

    def pass_flags(step):
        flag_copy(step).wait_recv()
        flags[step + 1] = jnp.maximum(flags[step], flags_in[step])
        if step + 1 < rounds:
            flag_copy(step + 1).start()

    def aside(sweep):
        for step in range(rounds):
            if min(step, SWEEPS - 1) == sweep:
                pass_flags(step)

    relaxation(acc, fields, weights, halo_out, halo_in, hsend_sem, hrecv_sem, surface_stage, smooth_stage, aside)
    full_out[0] = jnp.max(flags[rounds]).astype(jnp.int32)

    for step in range(rounds):
        flag_copy(step).wait_send()
    for side, there in ((0, has_above), (1, has_below)):

        @pl.when(there)
        def _(side=side):
            for k in range(others):
                node_copy(side, k).wait_send()
                for q in range(fit):
                    value_copy(side, k, q).wait_send()


def hand_over(surface, smooth, surface_out, smooth_out, out_sem):
    copies = [
        pltpu.make_async_copy(surface, surface_out, out_sem.at[0]),
        pltpu.make_async_copy(smooth, smooth_out, out_sem.at[1]),
    ]
    for copy in copies:
        copy.start()
    for copy in copies:
        copy.wait()


def body(sensitivity, owner, patch_count, neighbours, coupling):
    columns, faces = sensitivity.shape
    patches = neighbours.shape[0]
    span = patches * NODES
    rows = faces // LANES
    chunk = min(512, faces)
    chunks = faces // chunk
    highs = span // LOW
    hbm = pl.BlockSpec(memory_space=pltpu.HBM)
    vmem = pl.BlockSpec(memory_space=pltpu.VMEM)
    smem = pl.BlockSpec(memory_space=pltpu.SMEM)
    links = neighbours.T.shape
    out = jax.ShapeDtypeStruct((columns, span), jnp.float32)
    kept = pltpu.VMEM((columns, span), jnp.float32)
    dma = pltpu.SemaphoreType.DMA
    operands = (sensitivity, owner.reshape(rows, LANES), patch_count, neighbours.T, coupling.T)
    peers = lax.axis_size("surf")
    link_scratch = [pltpu.VMEM(links, jnp.int32), pltpu.VMEM(links, jnp.float32), dma((2,))]
    field_scratch = [
        pltpu.VMEM((highs * columns, LOW), jnp.float32),
        pltpu.VMEM((SWEEPS, patches + 2 * REACH, columns, NODES), jnp.float32),
        pltpu.VMEM((NOFF + 3, patches, 8, LANES), jnp.float32),
        pltpu.VMEM((16, LANES), jnp.float32),
        pltpu.VMEM((2, SWEEPS - 1, REACH, columns, NODES), jnp.bfloat16),
        pltpu.VMEM((2, SWEEPS - 1, REACH, columns, NODES), jnp.bfloat16),
    ]

    def hand(outputs):
        return pl.pallas_call(
            hand_over,
            out_shape=(out, out),
            in_specs=[vmem, vmem],
            out_specs=(hbm, hbm),
            scratch_shapes=[dma((2,))],
            compiler_params=pltpu.CompilerParams(vmem_limit_bytes=16 * 1024 * 1024),
        )(*outputs)

    def whole():
        return pl.pallas_call(
            functools.partial(kernel, chunk),
            out_shape=(kept, kept),
            in_specs=[hbm, hbm, smem, hbm, hbm],
            out_specs=(vmem, vmem),
            scratch_shapes=[
                *link_scratch,
                pltpu.VMEM((3, chunks, columns, chunk), jnp.bfloat16),
                pltpu.VMEM((3, rows, LANES), jnp.int32),
                pltpu.VMEM((highs * columns, chunk), jnp.bfloat16),
                pltpu.VMEM((LOW, chunk), jnp.bfloat16),
                *field_scratch,
                dma((2,)),
                dma((chunks,)),
                dma,
                dma((2, chunks)),
                dma((2, chunks)),
                dma((2,)),
                dma((2,)),
                dma((2, SWEEPS)),
                dma((2, SWEEPS)),
            ],
            compiler_params=pltpu.CompilerParams(
                collective_id=0, has_side_effects=True, vmem_limit_bytes=VMEM_LIMIT
            ),
        )(*operands)

    if faces % WIDE or highs & (highs - 1) or peers & (peers - 1):
        return hand(whole())

    owns, blocks, fit, rounds = faces // WIDE, faces // BLOCK, WIDE // SLOTS, peers.bit_length() - 1
    others = blocks // fit
    surface, smooth, full = pl.pallas_call(
        packed_kernel,
        out_shape=(kept, kept, jax.ShapeDtypeStruct((1,), jnp.int32)),
        in_specs=[hbm, hbm, smem, hbm, hbm],
        out_specs=(vmem, vmem, smem),
        scratch_shapes=[
            *link_scratch,
            pltpu.VMEM((owns + 2 * others, columns, WIDE), jnp.bfloat16),
            pltpu.VMEM((rows, LANES), jnp.int32),
            pltpu.VMEM((owns + 2 * others, WIDE // LANES, LANES), jnp.int32),
            pltpu.VMEM((2 * rows, LANES), jnp.float32),
            pltpu.VMEM((2, others, columns, WIDE), jnp.bfloat16),
            pltpu.VMEM((2, others, WIDE // LANES, LANES), jnp.int32),
            pltpu.VMEM((2, 2 * SLOTS, BLOCK), jnp.bfloat16),
            pltpu.VMEM((highs * columns, WIDE), jnp.bfloat16),
            pltpu.VMEM((LOW, WIDE), jnp.bfloat16),
            *field_scratch,
            pltpu.VMEM((rounds + 1, 8, LANES), jnp.float32),
            pltpu.VMEM((rounds, 8, LANES), jnp.float32),
            dma((owns,)),
            dma,
            dma((2, others, fit)),
            dma((2, others, fit)),
            dma((2, others)),
            dma((2, others)),
            dma((2, SWEEPS)),
            dma((2, SWEEPS)),
            dma((rounds,)),
            dma((rounds,)),
        ],
        compiler_params=pltpu.CompilerParams(collective_id=1, has_side_effects=True, vmem_limit_bytes=VMEM_LIMIT),
    )(*operands)
    _, surface, smooth = lax.while_loop(
        lambda state: state[0] != 0, lambda state: (jnp.int32(0), *hand(whole())), (full[0], *hand((surface, smooth)))
    )
    return surface, smooth


def solution(mesh):
    placed = (
        P(None, ("groups", "surf")),
        P(("groups", "surf")),
        P(("groups", "surf")),
        P(("groups", "surf"), None),
        P(("groups", "surf"), None),
    )
    return jax.shard_map(
        body,
        mesh=mesh,
        in_specs=placed,
        out_specs=(P(None, ("groups", "surf")), P(None, ("groups", "surf"))),
        check_vma=False,
    )
```

time: 45.3 us -> 38.7 us (0.85)
  the two profiles are of different devices: /device:TPU:11 before, /device:TPU:12 now
where the time goes in v2:
time: 38.7 us; the launch traced here: 38.6 us
  Pallas kernels  36.6 us (95%)
  between operations  1.35 us (3%)
  loops' own time  0.63 us (2%)
    pallas_call x1, Pallas kernels, body(): pl.pallas_call(packed_kernel, out_shape=(kept, kept, jax.ShapeDtypeStruct...  34.9 us
    pallas_call x1, Pallas kernels, hand(): pl.pallas_call(hand_over, out_shape=(out, out), in_specs=[vmem, vmem], ou...  1.68 us

profile of v2, /device:TPU:12, one launch (start us, length us, event | category | flops | bytes accessed | tf_op | source)
XLA Modules:
  0.0 38.6 jit_solution(619985054305037269)
XLA Ops:
  1.3 34.9 %shard_map.68 = (f32[96,4096]{1,0:T(8,128)S(1)}, f32[96,4096]{1,0:T(8,128)S(1)}, s32[1]{0:T(128)}) custom-call(bf16[96,4096]{1,0:T(8,128)(2,1)} %sens.1, s32[32,128]{1,0:T(8,128)} %bitcast.4, s32[1]{0:T(128)S(6)} %copy.17.count, s32[9,32]{1,0:T(8,128)} %bitcast.6, f32[9,32]{1,0:T(8,128)} %bitcast.8), custom_call_target="tpu_custom_call" | custom-call | tf_op jit(solution)/shard_map/pallas_call | solution.py:742
  36.2 0.0 copy-start
  36.2 0.0 copy-start.1
  36.2 0.0 copy-start.2
  36.2 0.0 copy-start.3
  36.2 1.7 %shard_map.69 = (f32[96,4096]{1,0:T(8,128)}, f32[96,4096]{1,0:T(8,128)}) custom-call(f32[96,4096]{1,0:T(8,128)S(1)} %get-tuple-element.52.surface, f32[96,4096]{1,0:T(8,128)S(1)} %get-tuple-element.53.smooth), custom_call_target="tpu_custom_call" | custom-call | tf_op jit(solution)/shard_map/pallas_call | solution.py:700
  37.9 0.0 copy-done
  37.9 0.0 copy-done.1
  37.9 0.0 copy-done.2
  37.9 0.0 copy-done.3
  37.9 0.6 %while.11 = (s32[]{:T(128)}, f32[96,4096]{1,0:T(8,128)}, f32[96,4096]{1,0:T(8,128)}, bf16[96,4096]{1,0:T(8,128)(2,1)S(1)}, s32[32,128]{1,0:T(8,128)S(1)}, /*inde...) while((s32[]{:T(128)}, f32[96,4096]{1,0:T(8,128)}, f32[96,4096]{1,0:T(8,128)}, bf16[96,4096]{1,0:T(8,128)(2,1)S(1)}, ...), condition=%region_1.0_spmd, body=%region_0.0_spmd | while | flops 1 | bytes 81 | solution.py:774
Async XLA Ops:
  36.2 1.7 %copy-start = (bf16[96,4096]{1,0:T(8,128)(2,1)S(1)}, bf16[96,4096]{1,0:T(8,128)(2,1)}, u32[]{:S(2)}) copy-start(bf16[96,4096]{1,0:T(8,128)(2,1)} %sens.1) | copy-start | bytes 2359300
  36.2 1.7 %copy-start.1 = (s32[4096]{0:T(1024)S(1)}, s32[4096]{0:T(1024)}, u32[]{:S(2)}) copy-start(s32[4096]{0:T(1024)} %param.8) | copy-start | bytes 49156
  36.2 1.7 %copy-start.2 = (s32[32,9]{0,1:T(8,128)S(1)}, s32[32,9]{0,1:T(8,128)}, u32[]{:S(2)}) copy-start(s32[32,9]{0,1:T(8,128)} %param.10) | copy-start | bytes 3460
  36.2 1.7 %copy-start.3 = (f32[32,9]{0,1:T(8,128)S(1)}, f32[32,9]{0,1:T(8,128)}, u32[]{:S(2)}) copy-start(f32[32,9]{0,1:T(8,128)} %param.11) | copy-start | bytes 3460

commit v3 on v2

--- a/solution.py
+++ b/solution.py
@@ -17,6 +17,9 @@
 BLOCK = 512
 SLOTS = 256
 WIDE = 1024
+GROUP = 48
+LEVELS = 32766.0
+TINY = 1e-33
 VMEM_LIMIT = 60 * 1024 * 1024
 smoothing = 1.5
 OFFSETS = [d for d in range(-REACH, REACH + 1) if d != 0]
@@ -61,70 +64,77 @@
             fields[sweep, pl.ds(patches + REACH, REACH)] = zero_halo
 
 
-def relaxation(acc, fields, weights, halo_out, halo_in, hsend_sem, hrecv_sem, surface_stage, smooth_stage, aside):
+def relaxation(acc, fields, weights, halos, surface_stage, smooth_stage, aside):
+    halo_out, halo_in, scale_out, scale_in, hsend_sem, hrecv_sem, ssend_sem, srecv_sem = halos
     columns = fields.shape[2]
     patches = fields.shape[1] - 2 * REACH
     highs = patches * NODES // LOW
+    groups = columns // GROUP
     position = lax.axis_index("surf")
     has_below = position > 0
     has_above = position < lax.axis_size("surf") - 1
 
-    def halo_copy(side, sweep):
+    def halo_copies(side, sweep, g):
         target = position + 1 if side == 0 else position - 1
-        if sweep == SWEEPS - 1:
-            source = patches if side == 0 else REACH
-            landing = 0 if side == 0 else patches + REACH
-            src, dst = fields.at[sweep, pl.ds(source, REACH)], fields.at[sweep, pl.ds(landing, REACH)]
-        else:
-            src, dst = halo_out.at[side, sweep], halo_in.at[side, sweep]
-        return pltpu.make_async_remote_copy(
-            src_ref=src,
-            dst_ref=dst,
-            send_sem=hsend_sem.at[side, sweep],
-            recv_sem=hrecv_sem.at[side, sweep],
-            device_id={"surf": target},
-            device_id_type=MESH,
-        )
-
-    def put_surface(h):
+        return [
+            pltpu.make_async_remote_copy(
+                src_ref=src.at[side, sweep, g],
+                dst_ref=dst.at[side, sweep, g],
+                send_sem=send.at[side, sweep, g],
+                recv_sem=recv.at[side, sweep, g],
+                device_id={"surf": target},
+                device_id_type=MESH,
+            )
+            for src, dst, send, recv in (
+                (scale_out, scale_in, ssend_sem, srecv_sem),
+                (halo_out, halo_in, hsend_sem, hrecv_sem),
+            )
+        ]
+
+    def put_surface(h, g):
+        rows = pl.ds(g * GROUP, GROUP)
         for half in range(LOW // NODES):
             p = h * (LOW // NODES) + half
-            patch = acc[pl.ds(h * columns, columns), pl.ds(half * NODES, NODES)]
+            patch = acc[pl.ds(h * columns + g * GROUP, GROUP), pl.ds(half * NODES, NODES)]
             patch = patch * weights[NOFF + 2, p, 0:1, :]
-            fields[0, REACH + p] = patch
-            surface_stage[:, pl.ds(p * NODES, NODES)] = patch
-
-    def send_halo(sweep):
+            fields[0, REACH + p, rows] = patch
+            surface_stage[rows, pl.ds(p * NODES, NODES)] = patch
+
+    def spread(tile):
+        return jnp.concatenate([tile] * (GROUP // 8), axis=0)[None]
+
+    def send_halo(sweep, g):
         for side, there in ((0, has_above), (1, has_below)):
 
             @pl.when(there)
             def _(side=side):
-                if sweep < SWEEPS - 1:
-                    first = patches if side == 0 else REACH
-                    halo_out[side, sweep] = fields[sweep, pl.ds(first, REACH)].astype(jnp.bfloat16)
-                halo_copy(side, sweep).start()
-
-    def wait_halo(sweep):
+                first = patches if side == 0 else REACH
+                patch = fields[sweep, pl.ds(first, REACH), pl.ds(g * GROUP, GROUP)]
+                size = jnp.abs(patch)
+                peak = functools.reduce(
+                    jnp.maximum, [size[q, 8 * n : 8 * n + 8] for q in range(REACH) for n in range(GROUP // 8)]
+                )
+                peak = jnp.maximum(peak, TINY)
+                scale_out[side, sweep, g] = peak * (1.0 / LEVELS)
+                code = jnp.floor(patch * spread(LEVELS / peak) + 0.5)
+                halo_out[side, sweep, g] = code.astype(jnp.int32).astype(jnp.int16)
+                for copy in halo_copies(side, sweep, g):
+                    copy.start()
+
+    def wait_halo(sweep, g):
         for side, there in ((0, has_below), (1, has_above)):
 
             @pl.when(there)
             def _(side=side):
-                halo_copy(side, sweep).wait_recv()
-                if sweep < SWEEPS - 1:
-                    first = 0 if side == 0 else patches + REACH
-                    fields[sweep, pl.ds(first, REACH)] = halo_in[side, sweep].astype(jnp.float32)
-
-    ends = REACH * NODES // LOW
-    for h in list(range(ends)) + list(range(highs - ends, highs)):
-        put_surface(h)
-    send_halo(0)
-    for h in range(ends, highs - ends):
-        put_surface(h)
-
-
-    def relax(sweep, first, count):
-        for group in range(0, columns, 8 * PAIR):
-            blocks = [pl.ds(group + 8 * k, 8) for k in range(PAIR)]
+                for copy in halo_copies(side, sweep, g):
+                    copy.wait_recv()
+                first = 0 if side == 0 else patches + REACH
+                code = halo_in[side, sweep, g].astype(jnp.int32).astype(jnp.float32)
+                fields[sweep, pl.ds(first, REACH), pl.ds(g * GROUP, GROUP)] = code * spread(scale_in[side, sweep, g])
+
+    def relax(sweep, g, first, count):
+        for low in range(g * GROUP, (g + 1) * GROUP, 8 * PAIR):
+            blocks = [pl.ds(low + 8 * k, 8) for k in range(PAIR)]
             window = [[fields[sweep, first + q, c, :] for q in range(2 * REACH)] for c in blocks]
             for at in range(count):
                 p = first + at
@@ -142,31 +152,44 @@
                     else:
                         fields[sweep + 1, p + REACH, c, :] = terms[0]
 
-    def relax_inner(sweep):
+    def relax_inner(sweep, g):
         def one(step, carry):
-            relax(sweep, REACH + step * BATCH, BATCH)
+            relax(sweep, g, REACH + step * BATCH, BATCH)
             return carry
 
         lax.fori_loop(0, (patches - 2 * REACH) // BATCH, one, 0)
+
+    ends = REACH * NODES // LOW
+    for g in range(groups):
+        for h in list(range(ends)) + list(range(highs - ends, highs)):
+            put_surface(h, g)
+        send_halo(0, g)
+    for h in range(ends, highs - ends):
+        for g in range(groups):
+            put_surface(h, g)
 
     for sweep in range(SWEEPS):
         last = sweep == SWEEPS - 1
         if last:
-            relax_inner(sweep)
+            for g in range(groups):
+                relax_inner(sweep, g)
         aside(sweep)
-        wait_halo(sweep)
-        relax(sweep, 0, REACH)
-        relax(sweep, patches - REACH, REACH)
-        if not last:
-            send_halo(sweep + 1)
-            relax_inner(sweep)
+        for g in range(groups):
+            wait_halo(sweep, g)
+            relax(sweep, g, 0, REACH)
+            relax(sweep, g, patches - REACH, REACH)
+            if not last:
+                send_halo(sweep + 1, g)
+                relax_inner(sweep, g)
 
     for side, there in ((0, has_above), (1, has_below)):
 
         @pl.when(there)
         def _(side=side):
             for sweep in range(SWEEPS):
-                halo_copy(side, sweep).wait_send()
+                for g in range(groups):
+                    for copy in halo_copies(side, sweep, g):
+                        copy.wait_send()
 
 
 def kernel(
@@ -191,6 +214,8 @@
     table,
     halo_out,
     halo_in,
+    scale_out,
+    scale_in,
     out_sem,
     load_sem,
     oload_sem,
@@ -200,6 +225,8 @@
     orecv_sem,
     hsend_sem,
     hrecv_sem,
+    ssend_sem,
+    srecv_sem,
 ):
     columns, faces = sens.shape
     patches = neighbours.shape[1]
@@ -360,9 +387,8 @@
 
     lax.fori_loop(0, 3 * chunks, step, 0)
 
-    relaxation(
-        acc, fields, weights, halo_out, halo_in, hsend_sem, hrecv_sem, surface_stage, smooth_stage, lambda sweep: None
-    )
+    halos = (halo_out, halo_in, scale_out, scale_in, hsend_sem, hrecv_sem, ssend_sem, srecv_sem)
+    relaxation(acc, fields, weights, halos, surface_stage, smooth_stage, lambda sweep: None)
 
     for side, there in ((0, has_above), (1, has_below)):
 
@@ -400,6 +426,8 @@
     table,
     halo_out,
     halo_in,
+    scale_out,
+    scale_in,
     flags,
     flags_in,
     load_sem,
@@ -410,6 +438,8 @@
     nrecv_sem,
     hsend_sem,
     hrecv_sem,
+    ssend_sem,
+    srecv_sem,
     fsend_sem,
     frecv_sem,
 ):
@@ -643,7 +673,8 @@
             if min(step, SWEEPS - 1) == sweep:
                 pass_flags(step)
 
-    relaxation(acc, fields, weights, halo_out, halo_in, hsend_sem, hrecv_sem, surface_stage, smooth_stage, aside)
+    halos = (halo_out, halo_in, scale_out, scale_in, hsend_sem, hrecv_sem, ssend_sem, srecv_sem)
+    relaxation(acc, fields, weights, halos, surface_stage, smooth_stage, aside)
     full_out[0] = jnp.max(flags[rounds]).astype(jnp.int32)
 
     for step in range(rounds):
@@ -692,8 +723,8 @@
         pltpu.VMEM((SWEEPS, patches + 2 * REACH, columns, NODES), jnp.float32),
         pltpu.VMEM((NOFF + 3, patches, 8, LANES), jnp.float32),
         pltpu.VMEM((16, LANES), jnp.float32),
-        pltpu.VMEM((2, SWEEPS - 1, REACH, columns, NODES), jnp.bfloat16),
-        pltpu.VMEM((2, SWEEPS - 1, REACH, columns, NODES), jnp.bfloat16),
+        *[pltpu.VMEM((2, SWEEPS, columns // GROUP, REACH, GROUP, NODES), jnp.int16)] * 2,
+        *[pltpu.VMEM((2, SWEEPS, columns // GROUP, 8, NODES), jnp.float32)] * 2,
     ]
 
     def hand(outputs):
@@ -726,8 +757,7 @@
                 dma((2, chunks)),
                 dma((2,)),
                 dma((2,)),
-                dma((2, SWEEPS)),
-                dma((2, SWEEPS)),
+                *[dma((2, SWEEPS, columns // GROUP))] * 4,
             ],
             compiler_params=pltpu.CompilerParams(
                 collective_id=0, has_side_effects=True, vmem_limit_bytes=VMEM_LIMIT
@@ -764,8 +794,7 @@
             dma((2, others, fit)),
             dma((2, others)),
             dma((2, others)),
-            dma((2, SWEEPS)),
-            dma((2, SWEEPS)),
+            *[dma((2, SWEEPS, columns // GROUP))] * 4,
             dma((rounds,)),
             dma((rounds,)),
         ],

time: 38.7 us -> 35.9 us (0.928)
  the two profiles are of different devices: /device:TPU:12 before, /device:TPU:11 now
where the time goes in v3:
time: 35.9 us; the launch traced here: 35.7 us
  Pallas kernels  33.4 us (93%)
  between operations  1.52 us (4%)
  loops' own time  0.81 us (2%)
    pallas_call x1, Pallas kernels, body(): pl.pallas_call(packed_kernel, out_shape=(kept, kept, jax.ShapeDtypeStruct...  31.7 us
    pallas_call x1, Pallas kernels, hand(): pl.pallas_call(hand_over, out_shape=(out, out), in_specs=[vmem, vmem], ou...  1.68 us
    another operation x1, loops' own time, body(): lax.while_loop(lambda state: state[0] != 0, lambda state: (jnp.int32(0),...  0.81 us

profile of v3, /device:TPU:11, one launch (start us, length us, event | category | flops | bytes accessed | tf_op | source)
XLA Modules:
  0.0 35.7 jit_solution(108644482368580807)
XLA Ops:
  1.3 31.7 %shard_map.68 = (f32[96,4096]{1,0:T(8,128)S(1)}, f32[96,4096]{1,0:T(8,128)S(1)}, s32[1]{0:T(128)}) custom-call(bf16[96,4096]{1,0:T(8,128)(2,1)} %sens.1, s32[32,128]{1,0:T(8,128)} %bitcast.4, s32[1]{0:T(128)S(6)} %copy.17.count, s32[9,32]{1,0:T(8,128)} %bitcast.6, f32[9,32]{1,0:T(8,128)} %bitcast.8), custom_call_target="tpu_custom_call" | custom-call | tf_op jit(solution)/shard_map/pallas_call | solution.py:772
  33.0 0.0 copy-start
  33.0 0.0 copy-start.1
  33.0 0.0 copy-start.2
  33.0 0.0 copy-start.3
  33.0 1.7 %shard_map.69 = (f32[96,4096]{1,0:T(8,128)}, f32[96,4096]{1,0:T(8,128)}) custom-call(f32[96,4096]{1,0:T(8,128)S(1)} %get-tuple-element.52.surface, f32[96,4096]{1,0:T(8,128)S(1)} %get-tuple-element.53.smooth), custom_call_target="tpu_custom_call" | custom-call | tf_op jit(solution)/shard_map/pallas_call | solution.py:731
  34.7 0.0 copy-done
  34.7 0.0 copy-done.1
  34.7 0.0 copy-done.2
  34.7 0.0 copy-done.3
  34.7 0.8 %while.11 = (s32[]{:T(128)}, f32[96,4096]{1,0:T(8,128)}, f32[96,4096]{1,0:T(8,128)}, bf16[96,4096]{1,0:T(8,128)(2,1)S(1)}, s32[32,128]{1,0:T(8,128)S(1)}, /*inde...) while((s32[]{:T(128)}, f32[96,4096]{1,0:T(8,128)}, f32[96,4096]{1,0:T(8,128)}, bf16[96,4096]{1,0:T(8,128)(2,1)S(1)}, ...), condition=%region_1.0_spmd, body=%region_0.0_spmd | while | flops 1 | bytes 81 | solution.py:803
Async XLA Ops:
  33.0 1.7 %copy-start = (bf16[96,4096]{1,0:T(8,128)(2,1)S(1)}, bf16[96,4096]{1,0:T(8,128)(2,1)}, u32[]{:S(2)}) copy-start(bf16[96,4096]{1,0:T(8,128)(2,1)} %sens.1) | copy-start | bytes 2359300
  33.0 1.7 %copy-start.1 = (s32[4096]{0:T(1024)S(1)}, s32[4096]{0:T(1024)}, u32[]{:S(2)}) copy-start(s32[4096]{0:T(1024)} %param.8) | copy-start | bytes 49156
  33.0 1.7 %copy-start.2 = (s32[32,9]{0,1:T(8,128)S(1)}, s32[32,9]{0,1:T(8,128)}, u32[]{:S(2)}) copy-start(s32[32,9]{0,1:T(8,128)} %param.10) | copy-start | bytes 3460
  33.0 1.7 %copy-start.3 = (f32[32,9]{0,1:T(8,128)S(1)}, f32[32,9]{0,1:T(8,128)}, u32[]{:S(2)}) copy-start(f32[32,9]{0,1:T(8,128)} %param.11) | copy-start | bytes 3460

commit v4 on v3

--- a/solution.py
+++ b/solution.py
@@ -17,6 +17,8 @@
 BLOCK = 512
 SLOTS = 256
 WIDE = 1024
+DEPTH = REACH * SWEEPS
+MARGIN = DEPTH - REACH
 GROUP = 48
 LEVELS = 32766.0
 TINY = 1e-33
@@ -27,11 +29,9 @@
 MESH = pl.DeviceIdType.MESH
 
 
-def prepare(count, neighbours, coupling, table, weights, fields):
-    patches, columns = neighbours.shape[1], fields.shape[2]
+def tabulate(count, neighbours, coupling, tables):
+    patches = neighbours.shape[1]
     position = lax.axis_index("surf")
-    has_below = position > 0
-    has_above = position < lax.axis_size("surf") - 1
     slots = lax.broadcasted_iota(jnp.int32, neighbours.shape, 1)
     distance = neighbours[...] - (position * patches + slots)
     links = coupling[...]
@@ -43,45 +43,80 @@
         for offset in OFFSETS
     ]
     lines += [share, smoothing * share, alive]
-    table[...] = jnp.zeros_like(table)
+    tables[0] = jnp.zeros(tables.shape[1:], jnp.float32)
     for at, line in enumerate(lines):
-        table[pl.ds(at, 1), pl.ds(0, patches)] = line
-    turned = jnp.transpose(table[...])
-    for at in range(len(lines)):
-        line = jnp.broadcast_to(turned[0:patches, at : at + 1], (patches, LANES))
-        weights[at] = jnp.broadcast_to(line[:, None, :], (patches, 8, LANES))
-
-    zero_halo = jnp.zeros((REACH, columns, NODES), jnp.float32)
-
-    @pl.when(jnp.logical_not(has_below))
-    def _():
-        for sweep in range(SWEEPS):
-            fields[sweep, pl.ds(0, REACH)] = zero_halo
-
-    @pl.when(jnp.logical_not(has_above))
-    def _():
-        for sweep in range(SWEEPS):
-            fields[sweep, pl.ds(patches + REACH, REACH)] = zero_halo
+        tables[0, pl.ds(at, 1), pl.ds(0, patches)] = line
+
+
+def table_copy(side, tables, send_sem, recv_sem):
+    position = lax.axis_index("surf")
+    return pltpu.make_async_remote_copy(
+        src_ref=tables.at[0],
+        dst_ref=tables.at[1 + side],
+        send_sem=send_sem.at[side],
+        recv_sem=recv_sem.at[side],
+        device_id={"surf": position + 1 if side == 0 else position - 1},
+        device_id_type=MESH,
+    )
+
+
+def send_tables(tables, send_sem, recv_sem):
+    position = lax.axis_index("surf")
+
+    @pl.when(position < lax.axis_size("surf") - 1)
+    def _():
+        table_copy(0, tables, send_sem, recv_sem).start()
+
+    @pl.when(position > 0)
+    def _():
+        table_copy(1, tables, send_sem, recv_sem).start()
+
+
+def prepare(tables, send_sem, recv_sem, weights, fields):
+    patches, columns = fields.shape[1] - 2 * DEPTH, fields.shape[2]
+    position = lax.axis_index("surf")
+    has_below = position > 0
+    has_above = position < lax.axis_size("surf") - 1
+    for side, there, landing in ((0, has_below, 0), (1, has_above, patches + DEPTH)):
+
+        @pl.when(there)
+        def _(side=side):
+            table_copy(side, tables, send_sem, recv_sem).wait_recv()
+
+        @pl.when(jnp.logical_not(there))
+        def _(side=side, landing=landing):
+            tables[1 + side] = jnp.zeros(tables.shape[1:], jnp.float32)
+            fields[0, pl.ds(landing, DEPTH)] = jnp.zeros((DEPTH, columns, NODES), jnp.float32)
+
+    at = lax.broadcasted_iota(jnp.int32, tables.shape[1:], 1)
+    below = pltpu.roll(tables[1], (MARGIN - patches) % LANES, 1)
+    own = pltpu.roll(tables[0], MARGIN, 1)
+    above = pltpu.roll(tables[2], MARGIN + patches, 1)
+    count = patches + 2 * MARGIN
+    table = jnp.where(at < MARGIN, below, jnp.where(at < MARGIN + patches, own, jnp.where(at < count, above, 0.0)))
+    turned = jnp.transpose(table)
+    for at in range(NOFF + 3):
+        line = jnp.broadcast_to(turned[0:count, at : at + 1], (count, LANES))
+        weights[at] = jnp.broadcast_to(line[:, None, :], (count, 8, LANES))
 
 
 def relaxation(acc, fields, weights, halos, surface_stage, smooth_stage, aside):
     halo_out, halo_in, scale_out, scale_in, hsend_sem, hrecv_sem, ssend_sem, srecv_sem = halos
     columns = fields.shape[2]
-    patches = fields.shape[1] - 2 * REACH
+    patches = fields.shape[1] - 2 * DEPTH
     highs = patches * NODES // LOW
     groups = columns // GROUP
     position = lax.axis_index("surf")
     has_below = position > 0
     has_above = position < lax.axis_size("surf") - 1
 
-    def halo_copies(side, sweep, g):
-        target = position + 1 if side == 0 else position - 1
+    def halo_copies(side, g, target):
         return [
             pltpu.make_async_remote_copy(
-                src_ref=src.at[side, sweep, g],
-                dst_ref=dst.at[side, sweep, g],
-                send_sem=send.at[side, sweep, g],
-                recv_sem=recv.at[side, sweep, g],
+                src_ref=src.at[side, g],
+                dst_ref=dst.at[side, g],
+                send_sem=send.at[side, g],
+                recv_sem=recv.at[side, g],
                 device_id={"surf": target},
                 device_id_type=MESH,
             )
@@ -96,100 +131,110 @@
         for half in range(LOW // NODES):
             p = h * (LOW // NODES) + half
             patch = acc[pl.ds(h * columns + g * GROUP, GROUP), pl.ds(half * NODES, NODES)]
-            patch = patch * weights[NOFF + 2, p, 0:1, :]
-            fields[0, REACH + p, rows] = patch
+            patch = patch * weights[NOFF + 2, MARGIN + p, 0:1, :]
+            fields[0, DEPTH + p, rows] = patch
             surface_stage[rows, pl.ds(p * NODES, NODES)] = patch
 
     def spread(tile):
         return jnp.concatenate([tile] * (GROUP // 8), axis=0)[None]
 
-    def send_halo(sweep, g):
-        for side, there in ((0, has_above), (1, has_below)):
+    def send_halo(g):
+        for side, there, first in ((0, has_above, patches), (1, has_below, DEPTH)):
 
             @pl.when(there)
-            def _(side=side):
-                first = patches if side == 0 else REACH
-                patch = fields[sweep, pl.ds(first, REACH), pl.ds(g * GROUP, GROUP)]
-                size = jnp.abs(patch)
-                peak = functools.reduce(
-                    jnp.maximum, [size[q, 8 * n : 8 * n + 8] for q in range(REACH) for n in range(GROUP // 8)]
-                )
-                peak = jnp.maximum(peak, TINY)
-                scale_out[side, sweep, g] = peak * (1.0 / LEVELS)
-                code = jnp.floor(patch * spread(LEVELS / peak) + 0.5)
-                halo_out[side, sweep, g] = code.astype(jnp.int32).astype(jnp.int16)
-                for copy in halo_copies(side, sweep, g):
+            def _(side=side, first=first):
+                for part in range(DEPTH // BATCH):
+                    patch = fields[0, pl.ds(first + part * BATCH, BATCH), pl.ds(g * GROUP, GROUP)]
+                    size = jnp.abs(patch)
+                    peak = functools.reduce(
+                        jnp.maximum, [size[q, 8 * n : 8 * n + 8] for q in range(BATCH) for n in range(GROUP // 8)]
+                    )
+                    peak = jnp.maximum(peak, TINY)
+                    scale_out[side, g, part] = peak * (1.0 / LEVELS)
+                    code = jnp.floor(patch * spread(LEVELS / peak) + 0.5)
+                    halo_out[side, g, pl.ds(part * BATCH, BATCH)] = code.astype(jnp.int32).astype(jnp.int16)
+                for copy in halo_copies(side, g, position + 1 if side == 0 else position - 1):
                     copy.start()
 
-    def wait_halo(sweep, g):
-        for side, there in ((0, has_below), (1, has_above)):
-
-            @pl.when(there)
-            def _(side=side):
-                for copy in halo_copies(side, sweep, g):
-                    copy.wait_recv()
-                first = 0 if side == 0 else patches + REACH
-                code = halo_in[side, sweep, g].astype(jnp.int32).astype(jnp.float32)
-                fields[sweep, pl.ds(first, REACH), pl.ds(g * GROUP, GROUP)] = code * spread(scale_in[side, sweep, g])
-
-    def relax(sweep, g, first, count):
+    def wait_halo(side, g):
+        @pl.when(jnp.logical_or(jnp.logical_and(side == 0, has_below), jnp.logical_and(side == 1, has_above)))
+        def _():
+            for copy in halo_copies(side, g, position - 1 + 2 * side):
+                copy.wait_recv()
+            for part in range(DEPTH // BATCH):
+                code = halo_in[side, g, pl.ds(part * BATCH, BATCH)].astype(jnp.int32).astype(jnp.float32)
+                landing = side * (patches + DEPTH) + part * BATCH
+                fields[0, pl.ds(landing, BATCH), pl.ds(g * GROUP, GROUP)] = code * spread(scale_in[side, g, part])
+
+    def relax(sweep, g, first):
         for low in range(g * GROUP, (g + 1) * GROUP, 8 * PAIR):
             blocks = [pl.ds(low + 8 * k, 8) for k in range(PAIR)]
-            window = [[fields[sweep, first + q, c, :] for q in range(2 * REACH)] for c in blocks]
-            for at in range(count):
+            window = [[fields[sweep, first + MARGIN + q, c, :] for q in range(2 * REACH)] for c in blocks]
+            for at in range(BATCH):
                 p = first + at
-                parts = [weights[line, p] for line in range(NOFF + 2)]
+                parts = [weights[line, p + MARGIN] for line in range(NOFF + 2)]
                 for k, c in enumerate(blocks):
-                    window[k].append(fields[sweep, p + 2 * REACH, c, :])
+                    window[k].append(fields[sweep, p + DEPTH + REACH, c, :])
                     here = window[k][at + REACH]
                     terms = [parts[line] * window[k][at + REACH + offset] for line, offset in enumerate(OFFSETS)]
-                    terms.append(parts[NOFF] * fields[0, p + REACH, c, :])
+                    terms.append(parts[NOFF] * fields[0, p + DEPTH, c, :])
                     terms.append(parts[NOFF + 1] * (pltpu.roll(here, 1, 1) + pltpu.roll(here, NODES - 1, 1)))
                     while len(terms) > 1:
                         terms = [sum(terms[n : n + 2][1:], terms[n]) for n in range(0, len(terms), 2)]
                     if sweep == SWEEPS - 1:
                         smooth_stage[c, pl.ds(pl.multiple_of(p * NODES, NODES), NODES)] = terms[0]
                     else:
-                        fields[sweep + 1, p + REACH, c, :] = terms[0]
-
-    def relax_inner(sweep, g):
+                        fields[sweep + 1, p + DEPTH, c, :] = terms[0]
+
+    def relax_range(sweep, g, first, count):
         def one(step, carry):
-            relax(sweep, g, REACH + step * BATCH, BATCH)
+            relax(sweep, g, first + step * BATCH)
             return carry
 
-        lax.fori_loop(0, (patches - 2 * REACH) // BATCH, one, 0)
-
-    ends = REACH * NODES // LOW
+        lax.fori_loop(0, count // BATCH, one, 0)
+
     for g in range(groups):
-        for h in list(range(ends)) + list(range(highs - ends, highs)):
+        for h in range(highs):
             put_surface(h, g)
-        send_halo(0, g)
-    for h in range(ends, highs - ends):
+        send_halo(g)
+
+    for g in range(groups):
+        for sweep in range(SWEEPS - 1):
+            edge = REACH * (sweep + 1)
+            relax_range(sweep, g, edge, patches - 2 * edge)
+    aside()
+
+    def turn(at, carry):
+        side = lax.rem(position + 1 + at, 2)
         for g in range(groups):
-            put_surface(h, g)
-
-    for sweep in range(SWEEPS):
-        last = sweep == SWEEPS - 1
-        if last:
-            for g in range(groups):
-                relax_inner(sweep, g)
-        aside(sweep)
-        for g in range(groups):
-            wait_halo(sweep, g)
-            relax(sweep, g, 0, REACH)
-            relax(sweep, g, patches - REACH, REACH)
-            if not last:
-                send_halo(sweep + 1, g)
-                relax_inner(sweep, g)
+            wait_halo(side, g)
+            for sweep in range(SWEEPS):
+                low = REACH * sweep - MARGIN
+                high = patches - REACH * (sweep + 1)
+                relax_range(sweep, g, low + side * (high - low), DEPTH)
+        return carry
+
+    lax.fori_loop(0, 2, turn, 0)
 
     for side, there in ((0, has_above), (1, has_below)):
 
         @pl.when(there)
         def _(side=side):
-            for sweep in range(SWEEPS):
-                for g in range(groups):
-                    for copy in halo_copies(side, sweep, g):
-                        copy.wait_send()
+            for g in range(groups):
+                for copy in halo_copies(side, g, position + 1 if side == 0 else position - 1):
+                    copy.wait_send()
+
+
+def wait_tables(tables, send_sem, recv_sem):
+    position = lax.axis_index("surf")
+
+    @pl.when(position < lax.axis_size("surf") - 1)
+    def _():
+        table_copy(0, tables, send_sem, recv_sem).wait_send()
+
+    @pl.when(position > 0)
+    def _():
+        table_copy(1, tables, send_sem, recv_sem).wait_send()
 
 
 def kernel(
@@ -211,7 +256,7 @@
     acc,
     fields,
     weights,
-    table,
+    tables,
     halo_out,
     halo_in,
     scale_out,
@@ -227,6 +272,8 @@
     hrecv_sem,
     ssend_sem,
     srecv_sem,
+    tsend_sem,
+    trecv_sem,
 ):
     columns, faces = sens.shape
     patches = neighbours.shape[1]
@@ -316,7 +363,9 @@
 
     for link_copy in link_copies:
         link_copy.wait()
-    prepare(count, neighbours, coupling, table, weights, fields)
+    tabulate(count, neighbours, coupling, tables)
+    send_tables(tables, tsend_sem, trecv_sem)
+    prepare(tables, tsend_sem, trecv_sem, weights, fields)
 
     acc[...] = jnp.zeros_like(acc)
     first_node = position * span
@@ -388,7 +437,8 @@
     lax.fori_loop(0, 3 * chunks, step, 0)
 
     halos = (halo_out, halo_in, scale_out, scale_in, hsend_sem, hrecv_sem, ssend_sem, srecv_sem)
-    relaxation(acc, fields, weights, halos, surface_stage, smooth_stage, lambda sweep: None)
+    relaxation(acc, fields, weights, halos, surface_stage, smooth_stage, lambda: None)
+    wait_tables(tables, tsend_sem, trecv_sem)
 
     for side, there in ((0, has_above), (1, has_below)):
 
@@ -423,7 +473,7 @@
     acc,
     fields,
     weights,
-    table,
+    tables,
     halo_out,
     halo_in,
     scale_out,
@@ -440,6 +490,8 @@
     hrecv_sem,
     ssend_sem,
     srecv_sem,
+    tsend_sem,
+    trecv_sem,
     fsend_sem,
     frecv_sem,
 ):
@@ -545,6 +597,9 @@
     over = jnp.where(leaves & (place > SLOTS - 0.5), 1.0, 0.0)
     flags[0] = functools.reduce(jnp.maximum, [over[8 * n : 8 * n + 8] for n in range(2 * rows // 8)])
 
+    for link_copy in link_copies:
+        link_copy.wait()
+    tabulate(count, neighbours, coupling, tables)
     both = jnp.logical_and(has_below, has_above)
 
     @pl.when(both)
@@ -556,6 +611,7 @@
         pl.semaphore_wait(barrier, 1 + rounds)
 
     flag_copy(0).start()
+    send_tables(tables, tsend_sem, trecv_sem)
     for k in range(owns):
         local_load(k).wait()
 
@@ -610,9 +666,6 @@
 
     lax.fori_loop(0, others, pack, 0)
 
-    for link_copy in link_copies:
-        link_copy.wait()
-    prepare(count, neighbours, coupling, table, weights, fields)
     acc[...] = jnp.zeros_like(acc)
 
     def add_chunk(s):
@@ -634,6 +687,19 @@
             masked[...], low_hot[...], (((1,), (1,)), ((), ())), preferred_element_type=jnp.float32
         )
 
+    def pass_flags(step):
+        flag_copy(step).wait_recv()
+        flags[step + 1] = jnp.maximum(flags[step], flags_in[step])
+        if step + 1 < rounds:
+            flag_copy(step + 1).start()
+
+    steps = owns + 2 * others
+    early = [r for r in range(rounds) if 2 * r + 2 < steps]
+
+    def aside():
+        for r in range(len(early), rounds):
+            pass_flags(r)
+
     def step(s, carry):
         t = jnp.maximum(s - owns, 0)
         side = lax.rem(t, 2)
@@ -642,6 +708,16 @@
         from_below = jnp.logical_and(jnp.logical_not(is_own), jnp.logical_and(side == 0, has_below))
         from_above = jnp.logical_and(jnp.logical_not(is_own), jnp.logical_and(side == 1, has_above))
 
+        for r in early:
+
+            @pl.when(s == 2 * r + 2)
+            def _(r=r):
+                pass_flags(r)
+
+        @pl.when(s == owns)
+        def _():
+            prepare(tables, tsend_sem, trecv_sem, weights, fields)
+
         @pl.when(from_below)
         def _():
             node_copy(0, k).wait_recv()
@@ -660,21 +736,11 @@
 
         return carry
 
-    lax.fori_loop(0, owns + 2 * others, step, 0)
-
-    def pass_flags(step):
-        flag_copy(step).wait_recv()
-        flags[step + 1] = jnp.maximum(flags[step], flags_in[step])
-        if step + 1 < rounds:
-            flag_copy(step + 1).start()
-
-    def aside(sweep):
-        for step in range(rounds):
-            if min(step, SWEEPS - 1) == sweep:
-                pass_flags(step)
+    lax.fori_loop(0, steps, step, 0)
 
     halos = (halo_out, halo_in, scale_out, scale_in, hsend_sem, hrecv_sem, ssend_sem, srecv_sem)
     relaxation(acc, fields, weights, halos, surface_stage, smooth_stage, aside)
+    wait_tables(tables, tsend_sem, trecv_sem)
     full_out[0] = jnp.max(flags[rounds]).astype(jnp.int32)
 
     for step in range(rounds):
@@ -720,11 +786,11 @@
     link_scratch = [pltpu.VMEM(links, jnp.int32), pltpu.VMEM(links, jnp.float32), dma((2,))]
     field_scratch = [
         pltpu.VMEM((highs * columns, LOW), jnp.float32),
-        pltpu.VMEM((SWEEPS, patches + 2 * REACH, columns, NODES), jnp.float32),
-        pltpu.VMEM((NOFF + 3, patches, 8, LANES), jnp.float32),
-        pltpu.VMEM((16, LANES), jnp.float32),
-        *[pltpu.VMEM((2, SWEEPS, columns // GROUP, REACH, GROUP, NODES), jnp.int16)] * 2,
-        *[pltpu.VMEM((2, SWEEPS, columns // GROUP, 8, NODES), jnp.float32)] * 2,
+        pltpu.VMEM((SWEEPS, patches + 2 * DEPTH, columns, NODES), jnp.float32),
+        pltpu.VMEM((NOFF + 3, patches + 2 * MARGIN, 8, LANES), jnp.float32),
+        pltpu.VMEM((3, 16, LANES), jnp.float32),
+        *[pltpu.VMEM((2, columns // GROUP, DEPTH, GROUP, NODES), jnp.int16)] * 2,
+        *[pltpu.VMEM((2, columns // GROUP, DEPTH // BATCH, 8, NODES), jnp.float32)] * 2,
     ]
 
     def hand(outputs):
@@ -757,7 +823,8 @@
                 dma((2, chunks)),
                 dma((2,)),
                 dma((2,)),
-                *[dma((2, SWEEPS, columns // GROUP))] * 4,
+                *[dma((2, columns // GROUP))] * 4,
+            *[dma((2,))] * 2,
             ],
             compiler_params=pltpu.CompilerParams(
                 collective_id=0, has_side_effects=True, vmem_limit_bytes=VMEM_LIMIT
@@ -794,7 +861,8 @@
             dma((2, others, fit)),
             dma((2, others)),
             dma((2, others)),
-            *[dma((2, SWEEPS, columns // GROUP))] * 4,
+            *[dma((2, columns // GROUP))] * 4,
+            *[dma((2,))] * 2,
             dma((rounds,)),
             dma((rounds,)),
         ],

time: 35.9 us -> 33.9 us (0.944)
  Pallas kernels: 33.4 us -> 31.7 us
    pallas_call x1, Pallas kernels: 31.7 us -> 30 us  [body(): pl.pallas_call(packed_kernel, out_shape=(kept, kept, jax.ShapeDtypeStruct...]
where the time goes in v4:
time: 33.9 us; the launch traced here: 33.7 us
  Pallas kernels  31.7 us (94%)
  between operations  1.35 us (4%)
  loops' own time  0.63 us (2%)
    pallas_call x1, Pallas kernels, body(): pl.pallas_call(packed_kernel, out_shape=(kept, kept, jax.ShapeDtypeStruct...  30 us
    pallas_call x1, Pallas kernels, hand(): pl.pallas_call(hand_over, out_shape=(out, out), in_specs=[vmem, vmem], ou...  1.68 us

profile of v4, /device:TPU:11, one launch (start us, length us, event | category | flops | bytes accessed | tf_op | source)
XLA Modules:
  0.0 33.7 jit_solution(13707285306706215172)
XLA Ops:
  1.3 30.0 %shard_map.68 = (f32[96,4096]{1,0:T(8,128)S(1)}, f32[96,4096]{1,0:T(8,128)S(1)}, s32[1]{0:T(128)}) custom-call(bf16[96,4096]{1,0:T(8,128)(2,1)} %sens.1, s32[32,128]{1,0:T(8,128)} %bitcast.4, s32[1]{0:T(128)S(6)} %copy.17.count, s32[9,32]{1,0:T(8,128)} %bitcast.6, f32[9,32]{1,0:T(8,128)} %bitcast.8), custom_call_target="tpu_custom_call" | custom-call | tf_op jit(solution)/shard_map/pallas_call | solution.py:839
  31.3 0.0 copy-start
  31.3 0.0 copy-start.1
  31.3 0.0 copy-start.2
  31.3 0.0 copy-start.3
  31.3 1.7 %shard_map.69 = (f32[96,4096]{1,0:T(8,128)}, f32[96,4096]{1,0:T(8,128)}) custom-call(f32[96,4096]{1,0:T(8,128)S(1)} %get-tuple-element.52.surface, f32[96,4096]{1,0:T(8,128)S(1)} %get-tuple-element.53.smooth), custom_call_target="tpu_custom_call" | custom-call | tf_op jit(solution)/shard_map/pallas_call | solution.py:797
  33.0 0.0 copy-done
  33.0 0.0 copy-done.1
  33.0 0.0 copy-done.2
  33.0 0.0 copy-done.3
  33.1 0.6 %while.11 = (s32[]{:T(128)}, f32[96,4096]{1,0:T(8,128)}, f32[96,4096]{1,0:T(8,128)}, bf16[96,4096]{1,0:T(8,128)(2,1)S(1)}, s32[32,128]{1,0:T(8,128)S(1)}, /*inde...) while((s32[]{:T(128)}, f32[96,4096]{1,0:T(8,128)}, f32[96,4096]{1,0:T(8,128)}, bf16[96,4096]{1,0:T(8,128)(2,1)S(1)}, ...), condition=%region_1.0_spmd, body=%region_0.0_spmd | while | flops 1 | bytes 81 | solution.py:871
Async XLA Ops:
  31.3 1.7 %copy-start = (bf16[96,4096]{1,0:T(8,128)(2,1)S(1)}, bf16[96,4096]{1,0:T(8,128)(2,1)}, u32[]{:S(2)}) copy-start(bf16[96,4096]{1,0:T(8,128)(2,1)} %sens.1) | copy-start | bytes 2359300
  31.3 1.7 %copy-start.1 = (s32[4096]{0:T(1024)S(1)}, s32[4096]{0:T(1024)}, u32[]{:S(2)}) copy-start(s32[4096]{0:T(1024)} %param.8) | copy-start | bytes 49156
  31.3 1.7 %copy-start.2 = (s32[32,9]{0,1:T(8,128)S(1)}, s32[32,9]{0,1:T(8,128)}, u32[]{:S(2)}) copy-start(s32[32,9]{0,1:T(8,128)} %param.10) | copy-start | bytes 3460
  31.3 1.7 %copy-start.3 = (f32[32,9]{0,1:T(8,128)S(1)}, f32[32,9]{0,1:T(8,128)}, u32[]{:S(2)}) copy-start(f32[32,9]{0,1:T(8,128)} %param.11) | copy-start | bytes 3460

commit v5 on v4

--- a/solution.py
+++ b/solution.py
@@ -20,6 +20,7 @@
 DEPTH = REACH * SWEEPS
 MARGIN = DEPTH - REACH
 GROUP = 48
+PART = 8
 LEVELS = 32766.0
 TINY = 1e-33
 VMEM_LIMIT = 60 * 1024 * 1024
@@ -100,7 +101,7 @@
         weights[at] = jnp.broadcast_to(line[:, None, :], (count, 8, LANES))
 
 
-def relaxation(acc, fields, weights, halos, surface_stage, smooth_stage, aside):
+def relaxation(acc, fields, weights, halos, surface_stage, smooth_stage, gather, aside):
     halo_out, halo_in, scale_out, scale_in, hsend_sem, hrecv_sem, ssend_sem, srecv_sem = halos
     columns = fields.shape[2]
     patches = fields.shape[1] - 2 * DEPTH
@@ -130,41 +131,40 @@
         rows = pl.ds(g * GROUP, GROUP)
         for half in range(LOW // NODES):
             p = h * (LOW // NODES) + half
-            patch = acc[pl.ds(h * columns + g * GROUP, GROUP), pl.ds(half * NODES, NODES)]
+            patch = acc[pl.ds(pl.multiple_of((g * highs + h) * GROUP, 8), GROUP), pl.ds(half * NODES, NODES)]
             patch = patch * weights[NOFF + 2, MARGIN + p, 0:1, :]
             fields[0, DEPTH + p, rows] = patch
-            surface_stage[rows, pl.ds(p * NODES, NODES)] = patch
+            surface_stage[rows, pl.ds(pl.multiple_of(p * NODES, NODES), NODES)] = patch
 
     def spread(tile):
         return jnp.concatenate([tile] * (GROUP // 8), axis=0)[None]
 
-    def send_halo(g):
-        for side, there, first in ((0, has_above, patches), (1, has_below, DEPTH)):
-
-            @pl.when(there)
-            def _(side=side, first=first):
-                for part in range(DEPTH // BATCH):
-                    patch = fields[0, pl.ds(first + part * BATCH, BATCH), pl.ds(g * GROUP, GROUP)]
-                    size = jnp.abs(patch)
-                    peak = functools.reduce(
-                        jnp.maximum, [size[q, 8 * n : 8 * n + 8] for q in range(BATCH) for n in range(GROUP // 8)]
-                    )
-                    peak = jnp.maximum(peak, TINY)
-                    scale_out[side, g, part] = peak * (1.0 / LEVELS)
-                    code = jnp.floor(patch * spread(LEVELS / peak) + 0.5)
-                    halo_out[side, g, pl.ds(part * BATCH, BATCH)] = code.astype(jnp.int32).astype(jnp.int16)
-                for copy in halo_copies(side, g, position + 1 if side == 0 else position - 1):
-                    copy.start()
+    def send_halo(side, g):
+        @pl.when(jnp.logical_or(jnp.logical_and(side == 0, has_above), jnp.logical_and(side == 1, has_below)))
+        def _():
+            first = patches + side * (DEPTH - patches)
+            for part in range(DEPTH // PART):
+                patch = fields[0, pl.ds(first + part * PART, PART), pl.ds(g * GROUP, GROUP)]
+                size = jnp.abs(patch)
+                peak = functools.reduce(
+                    jnp.maximum, [size[q, 8 * n : 8 * n + 8] for q in range(PART) for n in range(GROUP // 8)]
+                )
+                peak = jnp.maximum(peak, TINY)
+                scale_out[side, g, part] = peak * (1.0 / LEVELS)
+                code = jnp.floor(patch * spread(LEVELS / peak) + 0.5)
+                halo_out[side, g, pl.ds(part * PART, PART)] = code.astype(jnp.int32).astype(jnp.int16)
+            for copy in halo_copies(side, g, position + 1 - 2 * side):
+                copy.start()
 
     def wait_halo(side, g):
         @pl.when(jnp.logical_or(jnp.logical_and(side == 0, has_below), jnp.logical_and(side == 1, has_above)))
         def _():
             for copy in halo_copies(side, g, position - 1 + 2 * side):
                 copy.wait_recv()
-            for part in range(DEPTH // BATCH):
-                code = halo_in[side, g, pl.ds(part * BATCH, BATCH)].astype(jnp.int32).astype(jnp.float32)
-                landing = side * (patches + DEPTH) + part * BATCH
-                fields[0, pl.ds(landing, BATCH), pl.ds(g * GROUP, GROUP)] = code * spread(scale_in[side, g, part])
+            for part in range(DEPTH // PART):
+                code = halo_in[side, g, pl.ds(part * PART, PART)].astype(jnp.int32).astype(jnp.float32)
+                landing = side * (patches + DEPTH) + part * PART
+                fields[0, pl.ds(landing, PART), pl.ds(g * GROUP, GROUP)] = code * spread(scale_in[side, g, part])
 
     def relax(sweep, g, first):
         for low in range(g * GROUP, (g + 1) * GROUP, 8 * PAIR):
@@ -193,10 +193,22 @@
 
         lax.fori_loop(0, count // BATCH, one, 0)
 
+    ends = DEPTH * NODES // LOW
+
     for g in range(groups):
-        for h in range(highs):
+        gather(g)
+
+        def leave(at, carry, g=g):
+            side = lax.rem(position + 1 + at, 2)
+            for h in range(ends):
+                put_surface(h + (1 - side) * (highs - ends), g)
+            send_halo(side, g)
+            return carry
+
+        lax.fori_loop(0, 2, leave, 0)
+    for g in range(groups):
+        for h in range(ends, highs - ends):
             put_surface(h, g)
-        send_halo(g)
 
     for g in range(groups):
         for sweep in range(SWEEPS - 1):
@@ -381,9 +393,9 @@
             vals = values[slot, k, :, lanes]
             high_full = jnp.broadcast_to(high, vals.shape)
             for h in range(highs):
-                masked[pl.ds(h * columns, columns), lanes] = jnp.where(
-                    high_full == jnp.bfloat16(h), vals, jnp.bfloat16(0)
-                )
+                kept = jnp.where(high_full == jnp.bfloat16(h), vals, jnp.bfloat16(0))
+                for g in range(columns // GROUP):
+                    masked[pl.ds((g * highs + h) * GROUP, GROUP), lanes] = kept[g * GROUP : (g + 1) * GROUP]
         acc[...] += lax.dot_general(
             masked[...],
             low_hot[...],
@@ -437,7 +449,7 @@
     lax.fori_loop(0, 3 * chunks, step, 0)
 
     halos = (halo_out, halo_in, scale_out, scale_in, hsend_sem, hrecv_sem, ssend_sem, srecv_sem)
-    relaxation(acc, fields, weights, halos, surface_stage, smooth_stage, lambda: None)
+    relaxation(acc, fields, weights, halos, surface_stage, smooth_stage, lambda g: None, lambda: None)
     wait_tables(tables, tsend_sem, trecv_sem)
 
     for side, there in ((0, has_above), (1, has_below)):
@@ -447,6 +459,11 @@
             owner_copy(side).wait_send()
             for k in range(chunks):
                 face_copy(side, k).wait_send()
+
+
+def flag_masks(peers):
+    bits = peers.bit_length() - 1
+    return [[mask << at for mask in ((1, 2, 3) if at + 1 < bits else (1,))] for at in range(0, bits, 2)]
 
 
 def packed_kernel(
@@ -505,28 +522,33 @@
     pieces = WIDE // LANES
     fit = WIDE // SLOTS
     others = blocks // fit
+    groups = columns // GROUP
     position = lax.axis_index("surf")
     peers = lax.axis_size("surf")
-    rounds = peers.bit_length() - 1
+    masks = flag_masks(peers)
     has_below = position > 0
     has_above = position < peers - 1
     first_node = position * span
 
-    def partner(step):
-        size = 2 ** step
-        return position + size - 2 * size * (lax.div(position, size) % 2)
+    def partner(mask):
+        other = position
+        for bit in range(peers.bit_length()):
+            size = 2**bit
+            if mask & size:
+                other = other + size - 2 * size * (lax.div(position, size) % 2)
+        return other
 
     def local_load(k):
         return pltpu.make_async_copy(sens.at[:, pl.ds(k * WIDE, WIDE)], values.at[k], load_sem.at[k])
 
-    def value_copy(side, k, q):
+    def value_copy(side, k, q, g):
         target = position + 1 if side == 0 else position - 1
         lanes = pl.ds(pl.multiple_of(q * SLOTS, SLOTS), SLOTS)
         return pltpu.make_async_remote_copy(
-            src_ref=values_out.at[side, k, :, lanes],
-            dst_ref=values.at[owns + 2 * k + side, :, lanes],
-            send_sem=send_sem.at[side, k, q],
-            recv_sem=recv_sem.at[side, k, q],
+            src_ref=values_out.at[side, k, pl.ds(g * GROUP, GROUP), lanes],
+            dst_ref=values.at[owns + 2 * k + side, pl.ds(g * GROUP, GROUP), lanes],
+            send_sem=send_sem.at[side, k, q, g],
+            recv_sem=recv_sem.at[side, k, q, g],
             device_id={"surf": target},
             device_id_type=MESH,
         )
@@ -542,15 +564,18 @@
             device_id_type=MESH,
         )
 
-    def flag_copy(step):
-        return pltpu.make_async_remote_copy(
-            src_ref=flags.at[step],
-            dst_ref=flags_in.at[step],
-            send_sem=fsend_sem.at[step],
-            recv_sem=frecv_sem.at[step],
-            device_id={"surf": partner(step)},
-            device_id_type=MESH,
-        )
+    def flag_copies(step):
+        return [
+            pltpu.make_async_remote_copy(
+                src_ref=flags.at[step],
+                dst_ref=flags_in.at[step, n],
+                send_sem=fsend_sem.at[step, n],
+                recv_sem=frecv_sem.at[step, n],
+                device_id={"surf": partner(mask)},
+                device_id_type=MESH,
+            )
+            for n, mask in enumerate(masks[step])
+        ]
 
     own_owner = pltpu.make_async_copy(owner, owners, oload_sem)
     own_owner.start()
@@ -573,8 +598,9 @@
     def _():
         pl.semaphore_signal(barrier, inc=1, device_id={"surf": position + 1}, device_id_type=MESH)
 
-    for step in range(rounds):
-        pl.semaphore_signal(barrier, inc=1, device_id={"surf": partner(step)}, device_id_type=MESH)
+    greeted = [mask for step in masks for mask in step]
+    for mask in greeted:
+        pl.semaphore_signal(barrier, inc=1, device_id={"surf": partner(mask)}, device_id_type=MESH)
 
     own_owner.wait()
     local = owners[...] - first_node
@@ -604,13 +630,14 @@
 
     @pl.when(both)
     def _():
-        pl.semaphore_wait(barrier, 2 + rounds)
+        pl.semaphore_wait(barrier, 2 + len(greeted))
 
     @pl.when(jnp.logical_not(both))
     def _():
-        pl.semaphore_wait(barrier, 1 + rounds)
-
-    flag_copy(0).start()
+        pl.semaphore_wait(barrier, 1 + len(greeted))
+
+    for copy in flag_copies(0):
+        copy.start()
     send_tables(tables, tsend_sem, trecv_sem)
     for k in range(owns):
         local_load(k).wait()
@@ -654,7 +681,7 @@
 
                 @pl.when(there)
                 def _(side=side, q=q):
-                    value_copy(side, k, q).start()
+                    value_copy(side, k, q, 0).start()
 
         for side, there in ((0, has_above), (1, has_below)):
 
@@ -666,9 +693,22 @@
 
     lax.fori_loop(0, others, pack, 0)
 
+    def send_more(k, carry):
+        for side, there in ((0, has_above), (1, has_below)):
+
+            @pl.when(there)
+            def _(side=side):
+                for g in range(1, groups):
+                    for q in range(fit):
+                        value_copy(side, k, q, g).start()
+
+        return carry
+
+    lax.fori_loop(0, others, send_more, 0)
+
     acc[...] = jnp.zeros_like(acc)
 
-    def add_chunk(s):
+    def add_chunk(s, g):
         for j in range(pieces):
             node = nodes[s, pl.ds(j, 1), :]
             high = (node >> 8).astype(jnp.float32).astype(jnp.bfloat16)
@@ -677,74 +717,79 @@
             low_hot[:, lanes] = jnp.where(
                 slot_rows == jnp.broadcast_to(low, (LOW, LANES)), jnp.bfloat16(1), jnp.bfloat16(0)
             )
-            vals = values[s, :, lanes]
+            vals = values[s, pl.ds(g * GROUP, GROUP), lanes]
             high_full = jnp.broadcast_to(high, vals.shape)
             for h in range(highs):
-                masked[pl.ds(h * columns, columns), lanes] = jnp.where(
+                masked[pl.ds(h * GROUP, GROUP), lanes] = jnp.where(
                     high_full == jnp.bfloat16(h), vals, jnp.bfloat16(0)
                 )
-        acc[...] += lax.dot_general(
+        acc[pl.ds(g * highs * GROUP, highs * GROUP)] += lax.dot_general(
             masked[...], low_hot[...], (((1,), (1,)), ((), ())), preferred_element_type=jnp.float32
         )
 
     def pass_flags(step):
-        flag_copy(step).wait_recv()
-        flags[step + 1] = jnp.maximum(flags[step], flags_in[step])
-        if step + 1 < rounds:
-            flag_copy(step + 1).start()
-
-    steps = owns + 2 * others
-    early = [r for r in range(rounds) if 2 * r + 2 < steps]
+        total = flags[step]
+        for n, copy in enumerate(flag_copies(step)):
+            copy.wait_recv()
+            total = jnp.maximum(total, flags_in[step, n])
+        flags[step + 1] = total
+        if step + 1 < len(masks):
+            for copy in flag_copies(step + 1):
+                copy.start()
 
     def aside():
-        for r in range(len(early), rounds):
-            pass_flags(r)
-
-    def step(s, carry):
+        for step in range(1, len(masks) - 1):
+            pass_flags(step)
+
+    def step(g, s, carry):
         t = jnp.maximum(s - owns, 0)
-        side = lax.rem(t, 2)
-        k = lax.div(t, 2)
+        side = lax.rem(position + 1 + lax.div(t, others), 2)
+        k = lax.rem(t, others)
         is_own = s < owns
+        slot = jnp.where(is_own, s, owns + 2 * k + side)
         from_below = jnp.logical_and(jnp.logical_not(is_own), jnp.logical_and(side == 0, has_below))
         from_above = jnp.logical_and(jnp.logical_not(is_own), jnp.logical_and(side == 1, has_above))
 
-        for r in early:
-
-            @pl.when(s == 2 * r + 2)
-            def _(r=r):
-                pass_flags(r)
-
-        @pl.when(s == owns)
-        def _():
-            prepare(tables, tsend_sem, trecv_sem, weights, fields)
+        if g == 0:
+
+            @pl.when(s == owns)
+            def _():
+                if len(masks) > 1:
+                    pass_flags(0)
+                prepare(tables, tsend_sem, trecv_sem, weights, fields)
 
         @pl.when(from_below)
         def _():
-            node_copy(0, k).wait_recv()
+            if g == 0:
+                node_copy(0, k).wait_recv()
             for q in range(fit):
-                value_copy(0, k, q).wait_recv()
+                value_copy(0, k, q, g).wait_recv()
 
         @pl.when(from_above)
         def _():
-            node_copy(1, k).wait_recv()
+            if g == 0:
+                node_copy(1, k).wait_recv()
             for q in range(fit):
-                value_copy(1, k, q).wait_recv()
+                value_copy(1, k, q, g).wait_recv()
 
         @pl.when(jnp.logical_or(is_own, jnp.logical_or(from_below, from_above)))
         def _():
-            add_chunk(s)
+            add_chunk(slot, g)
 
         return carry
 
-    lax.fori_loop(0, steps, step, 0)
+    def gather(g):
+        lax.fori_loop(0, owns + 2 * others, functools.partial(step, g), 0)
 
     halos = (halo_out, halo_in, scale_out, scale_in, hsend_sem, hrecv_sem, ssend_sem, srecv_sem)
-    relaxation(acc, fields, weights, halos, surface_stage, smooth_stage, aside)
+    relaxation(acc, fields, weights, halos, surface_stage, smooth_stage, gather, aside)
     wait_tables(tables, tsend_sem, trecv_sem)
-    full_out[0] = jnp.max(flags[rounds]).astype(jnp.int32)
-
-    for step in range(rounds):
-        flag_copy(step).wait_send()
+    pass_flags(len(masks) - 1)
+    full_out[0] = jnp.max(flags[len(masks)]).astype(jnp.int32)
+
+    for step in range(len(masks)):
+        for copy in flag_copies(step):
+            copy.wait_send()
     for side, there in ((0, has_above), (1, has_below)):
 
         @pl.when(there)
@@ -752,7 +797,8 @@
             for k in range(others):
                 node_copy(side, k).wait_send()
                 for q in range(fit):
-                    value_copy(side, k, q).wait_send()
+                    for g in range(groups):
+                        value_copy(side, k, q, g).wait_send()
 
 
 def hand_over(surface, smooth, surface_out, smooth_out, out_sem):
@@ -790,7 +836,7 @@
         pltpu.VMEM((NOFF + 3, patches + 2 * MARGIN, 8, LANES), jnp.float32),
         pltpu.VMEM((3, 16, LANES), jnp.float32),
         *[pltpu.VMEM((2, columns // GROUP, DEPTH, GROUP, NODES), jnp.int16)] * 2,
-        *[pltpu.VMEM((2, columns // GROUP, DEPTH // BATCH, 8, NODES), jnp.float32)] * 2,
+        *[pltpu.VMEM((2, columns // GROUP, DEPTH // PART, 8, NODES), jnp.float32)] * 2,
     ]
 
     def hand(outputs):
@@ -831,10 +877,10 @@
             ),
         )(*operands)
 
-    if faces % WIDE or highs & (highs - 1) or peers & (peers - 1):
+    if faces % WIDE or highs & (highs - 1) or peers & (peers - 1) or peers < 2:
         return hand(whole())
 
-    owns, blocks, fit, rounds = faces // WIDE, faces // BLOCK, WIDE // SLOTS, peers.bit_length() - 1
+    owns, blocks, fit, rounds = faces // WIDE, faces // BLOCK, WIDE // SLOTS, len(flag_masks(peers))
     others = blocks // fit
     surface, smooth, full = pl.pallas_call(
         packed_kernel,
@@ -850,21 +896,21 @@
             pltpu.VMEM((2, others, columns, WIDE), jnp.bfloat16),
             pltpu.VMEM((2, others, WIDE // LANES, LANES), jnp.int32),
             pltpu.VMEM((2, 2 * SLOTS, BLOCK), jnp.bfloat16),
-            pltpu.VMEM((highs * columns, WIDE), jnp.bfloat16),
+            pltpu.VMEM((highs * GROUP, WIDE), jnp.bfloat16),
             pltpu.VMEM((LOW, WIDE), jnp.bfloat16),
             *field_scratch,
             pltpu.VMEM((rounds + 1, 8, LANES), jnp.float32),
-            pltpu.VMEM((rounds, 8, LANES), jnp.float32),
+            pltpu.VMEM((rounds, 3, 8, LANES), jnp.float32),
             dma((owns,)),
             dma,
-            dma((2, others, fit)),
-            dma((2, others, fit)),
+            dma((2, others, fit, columns // GROUP)),
+            dma((2, others, fit, columns // GROUP)),
             dma((2, others)),
             dma((2, others)),
             *[dma((2, columns // GROUP))] * 4,
             *[dma((2,))] * 2,
-            dma((rounds,)),
-            dma((rounds,)),
+            dma((rounds, 3)),
+            dma((rounds, 3)),
         ],
         compiler_params=pltpu.CompilerParams(collective_id=1, has_side_effects=True, vmem_limit_bytes=VMEM_LIMIT),
     )(*operands)

time: 33.9 us -> 32.8 us (0.968)
  Pallas kernels: 31.7 us -> 30.5 us
    pallas_call x1, Pallas kernels: 30 us -> 28.8 us  [body(): pl.pallas_call(packed_kernel, out_shape=(kept, kept, jax.ShapeDtypeStruct...]
where the time goes in v5:
time: 32.8 us; the launch traced here: 32.5 us
  Pallas kernels  30.5 us (93%)
  between operations  1.35 us (4%)
  loops' own time  0.63 us (2%)
    pallas_call x1, Pallas kernels, body(): pl.pallas_call(packed_kernel, out_shape=(kept, kept, jax.ShapeDtypeStruct...  28.8 us
    pallas_call x1, Pallas kernels, hand(): pl.pallas_call(hand_over, out_shape=(out, out), in_specs=[vmem, vmem], ou...  1.68 us

profile of v5, /device:TPU:11, one launch (start us, length us, event | category | flops | bytes accessed | tf_op | source)
XLA Modules:
  0.0 32.5 jit_solution(10433007655397651312)
XLA Ops:
  1.3 28.8 %shard_map.68 = (f32[96,4096]{1,0:T(8,128)S(1)}, f32[96,4096]{1,0:T(8,128)S(1)}, s32[1]{0:T(128)}) custom-call(bf16[96,4096]{1,0:T(8,128)(2,1)} %sens.1, s32[32,128]{1,0:T(8,128)} %bitcast.4, s32[1]{0:T(128)S(6)} %copy.17.count, s32[9,32]{1,0:T(8,128)} %bitcast.6, f32[9,32]{1,0:T(8,128)} %bitcast.8), custom_call_target="tpu_custom_call" | custom-call | tf_op jit(solution)/shard_map/pallas_call | solution.py:885
  30.1 0.0 copy-start
  30.1 0.0 copy-start.1
  30.1 0.0 copy-start.2
  30.1 0.0 copy-start.3
  30.1 1.7 %shard_map.69 = (f32[96,4096]{1,0:T(8,128)}, f32[96,4096]{1,0:T(8,128)}) custom-call(f32[96,4096]{1,0:T(8,128)S(1)} %get-tuple-element.52.surface, f32[96,4096]{1,0:T(8,128)S(1)} %get-tuple-element.53.smooth), custom_call_target="tpu_custom_call" | custom-call | tf_op jit(solution)/shard_map/pallas_call | solution.py:843
  31.8 0.0 copy-done
  31.8 0.0 copy-done.1
  31.9 0.0 copy-done.2
  31.9 0.0 copy-done.3
  31.9 0.6 %while.11 = (s32[]{:T(128)}, f32[96,4096]{1,0:T(8,128)}, f32[96,4096]{1,0:T(8,128)}, bf16[96,4096]{1,0:T(8,128)(2,1)S(1)}, s32[32,128]{1,0:T(8,128)S(1)}, /*inde...) while((s32[]{:T(128)}, f32[96,4096]{1,0:T(8,128)}, f32[96,4096]{1,0:T(8,128)}, bf16[96,4096]{1,0:T(8,128)(2,1)S(1)}, ...), condition=%region_1.0_spmd, body=%region_0.0_spmd | while | flops 1 | bytes 81 | solution.py:917
Async XLA Ops:
  30.1 1.7 %copy-start = (bf16[96,4096]{1,0:T(8,128)(2,1)S(1)}, bf16[96,4096]{1,0:T(8,128)(2,1)}, u32[]{:S(2)}) copy-start(bf16[96,4096]{1,0:T(8,128)(2,1)} %sens.1) | copy-start | bytes 2359300
  30.1 1.7 %copy-start.1 = (s32[4096]{0:T(1024)S(1)}, s32[4096]{0:T(1024)}, u32[]{:S(2)}) copy-start(s32[4096]{0:T(1024)} %param.8) | copy-start | bytes 49156
  30.1 1.7 %copy-start.2 = (s32[32,9]{0,1:T(8,128)S(1)}, s32[32,9]{0,1:T(8,128)}, u32[]{:S(2)}) copy-start(s32[32,9]{0,1:T(8,128)} %param.10) | copy-start | bytes 3460
  30.1 1.7 %copy-start.3 = (f32[32,9]{0,1:T(8,128)S(1)}, f32[32,9]{0,1:T(8,128)}, u32[]{:S(2)}) copy-start(f32[32,9]{0,1:T(8,128)} %param.11) | copy-start | bytes 3460

commit v6 on v5

--- a/solution.py
+++ b/solution.py
@@ -16,7 +16,7 @@
 BATCH = 8
 BLOCK = 512
 SLOTS = 256
-WIDE = 1024
+WIDE = 2048
 DEPTH = REACH * SWEEPS
 MARGIN = DEPTH - REACH
 GROUP = 48
@@ -166,11 +166,11 @@
                 landing = side * (patches + DEPTH) + part * PART
                 fields[0, pl.ds(landing, PART), pl.ds(g * GROUP, GROUP)] = code * spread(scale_in[side, g, part])
 
-    def relax(sweep, g, first):
+    def relax(sweep, g, first, batch):
         for low in range(g * GROUP, (g + 1) * GROUP, 8 * PAIR):
             blocks = [pl.ds(low + 8 * k, 8) for k in range(PAIR)]
             window = [[fields[sweep, first + MARGIN + q, c, :] for q in range(2 * REACH)] for c in blocks]
-            for at in range(BATCH):
+            for at in range(batch):
                 p = first + at
                 parts = [weights[line, p + MARGIN] for line in range(NOFF + 2)]
                 for k, c in enumerate(blocks):
@@ -188,7 +188,7 @@
 
     def relax_range(sweep, g, first, count):
         def one(step, carry):
-            relax(sweep, g, first + step * BATCH)
+            relax(sweep, g, first + step * BATCH, BATCH)
             return carry
 
         lax.fori_loop(0, count // BATCH, one, 0)
@@ -223,7 +223,7 @@
             for sweep in range(SWEEPS):
                 low = REACH * sweep - MARGIN
                 high = patches - REACH * (sweep + 1)
-                relax_range(sweep, g, low + side * (high - low), DEPTH)
+                relax(sweep, g, low + side * (high - low), DEPTH)
         return carry
 
     lax.fori_loop(0, 2, turn, 0)

time: 32.8 us -> 32.3 us (0.985)
  Pallas kernels: 30.5 us -> 29.7 us
    pallas_call x1, Pallas kernels: 28.8 us -> 28 us  [body(): pl.pallas_call(packed_kernel, out_shape=(kept, kept, jax.ShapeDtypeStruct...]
where the time goes in v6:
time: 32.3 us; the launch traced here: 32.1 us
  Pallas kernels  29.7 us (92%)
  between operations  1.52 us (5%)
  loops' own time  0.81 us (3%)
    pallas_call x1, Pallas kernels, body(): pl.pallas_call(packed_kernel, out_shape=(kept, kept, jax.ShapeDtypeStruct...  28 us
    pallas_call x1, Pallas kernels, hand(): pl.pallas_call(hand_over, out_shape=(out, out), in_specs=[vmem, vmem], ou...  1.68 us
    another operation x1, loops' own time, body(): lax.while_loop(lambda state: state[0] != 0, lambda state: (jnp.int32(0),...  0.81 us

profile of v6, /device:TPU:11, one launch (start us, length us, event | category | flops | bytes accessed | tf_op | source)
XLA Modules:
  0.0 32.1 jit_solution(474572178740400231)
XLA Ops:
  1.3 28.0 %shard_map.68 = (f32[96,4096]{1,0:T(8,128)S(1)}, f32[96,4096]{1,0:T(8,128)S(1)}, s32[1]{0:T(128)}) custom-call(bf16[96,4096]{1,0:T(8,128)(2,1)} %sens.1, s32[32,128]{1,0:T(8,128)} %bitcast.4, s32[1]{0:T(128)S(6)} %copy.17.count, s32[9,32]{1,0:T(8,128)} %bitcast.6, f32[9,32]{1,0:T(8,128)} %bitcast.8), custom_call_target="tpu_custom_call" | custom-call | tf_op jit(solution)/shard_map/pallas_call | solution.py:885
  29.3 0.0 copy-start
  29.3 0.0 copy-start.1
  29.4 0.0 copy-start.2
  29.4 0.0 copy-start.3
  29.4 1.7 %shard_map.69 = (f32[96,4096]{1,0:T(8,128)}, f32[96,4096]{1,0:T(8,128)}) custom-call(f32[96,4096]{1,0:T(8,128)S(1)} %get-tuple-element.52.surface, f32[96,4096]{1,0:T(8,128)S(1)} %get-tuple-element.53.smooth), custom_call_target="tpu_custom_call" | custom-call | tf_op jit(solution)/shard_map/pallas_call | solution.py:843
  31.1 0.0 copy-done
  31.1 0.0 copy-done.1
  31.1 0.0 copy-done.2
  31.1 0.0 copy-done.3
  31.1 0.8 %while.11 = (s32[]{:T(128)}, f32[96,4096]{1,0:T(8,128)}, f32[96,4096]{1,0:T(8,128)}, bf16[96,4096]{1,0:T(8,128)(2,1)S(1)}, s32[32,128]{1,0:T(8,128)S(1)}, /*inde...) while((s32[]{:T(128)}, f32[96,4096]{1,0:T(8,128)}, f32[96,4096]{1,0:T(8,128)}, bf16[96,4096]{1,0:T(8,128)(2,1)S(1)}, ...), condition=%region_1.0_spmd, body=%region_0.0_spmd | while | flops 1 | bytes 81 | solution.py:917
Async XLA Ops:
  29.3 1.7 %copy-start = (bf16[96,4096]{1,0:T(8,128)(2,1)S(1)}, bf16[96,4096]{1,0:T(8,128)(2,1)}, u32[]{:S(2)}) copy-start(bf16[96,4096]{1,0:T(8,128)(2,1)} %sens.1) | copy-start | bytes 2359300
  29.3 1.7 %copy-start.1 = (s32[4096]{0:T(1024)S(1)}, s32[4096]{0:T(1024)}, u32[]{:S(2)}) copy-start(s32[4096]{0:T(1024)} %param.8) | copy-start | bytes 49156
  29.4 1.7 %copy-start.2 = (s32[32,9]{0,1:T(8,128)S(1)}, s32[32,9]{0,1:T(8,128)}, u32[]{:S(2)}) copy-start(s32[32,9]{0,1:T(8,128)} %param.10) | copy-start | bytes 3460
  29.4 1.7 %copy-start.3 = (f32[32,9]{0,1:T(8,128)S(1)}, f32[32,9]{0,1:T(8,128)}, u32[]{:S(2)}) copy-start(f32[32,9]{0,1:T(8,128)} %param.11) | copy-start | bytes 3460
